TPU v7x, 128 devices: a whole 4x4x4 slice. The times are simulated.
128 devices in a mesh: gx: 32 (over y, x, core), gy: 4 (over z).
Axes of the slice: x: 4, y: 4, z: 4, core: 2. Of those that a mesh axis runs over, the one named last changes fastest.
Arguments:
- charges: float32 [8192, 256], P(('gx', 'gy')), may hold values from -6 to 6
- points: float32 [8192, 3, 256], P(('gx', 'gy')), may hold values from 0 to 2
- leaf_bases: float32 [8192, 256, 64], P(('gx', 'gy')), may hold values from -0.75 to 0.75
- leaf_transfer: float32 [8192, 64, 64], P(('gx', 'gy')), may hold values from -0.75 to 0.75
- near_target: int32 [8192, 8], P(('gx', 'gy')), may hold values from -1 to 8191, as said below
- far_target: int32 [8192, 16], P(('gx', 'gy')), may hold values from -1 to 8191, as said below
- leaf_coupling: float32 [8192, 16, 64, 64], P(('gx', 'gy')), may hold values from -0.1875 to 0.1875
- cluster_transfer: float32 [128, 64, 64], P(('gx', 'gy')), may hold values from -0.75 to 0.75
- cluster_target: int32 [128, 8], P(('gx', 'gy')), may hold values from -1 to 127, as said below
- cluster_coupling: float32 [128, 8, 64, 64], P(('gx', 'gy')), may hold values from -0.03125 to 0.03125
- group_transfer: float32 [32, 64, 64], replicated, may hold values from -0.75 to 0.75
- group_target: int32 [32, 8], P('gx'), may hold values from -1 to 31, as said below
- group_coupling: float32 [32, 8, 64, 64], P('gx'), may hold values from -0.015625 to 0.015625
- top_target: int32 [8, 4], replicated, may hold values from -1 to 7, as said below
- top_coupling: float32 [8, 4, 64, 64], replicated, may hold values from -0.01171875 to 0.01171875
Outputs:
- potential: float32 [8192, 256], P(('gx', 'gy'))
Inputs may be any that keep to these rules, and one draw needn't show every extreme that they name: `near_target`: live slots of a row come first. A live target of leaf i lies among the leaves of i's own device cluster and of the device clusters just before and after it. `far_target`: live slots of a row come first. A live target of leaf i lies among the leaves of the device clusters at most 2 before or after i's own. `cluster_target`: live slots of a row come first. `group_target`: live slots of a row come first. `top_target`: live slots of a row come first.
All inputs are finite; a program needn't handle non-finite values.
Results may differ from a plain program's by a relative error of at most 0.00012.
Values sent between devices are 32-bit elements; how exact they have to be, the bound alone decides.
A program may use at most 128 MiB of HBM per device.

v0:
```python
import functools
import math

import jax
import jax.numpy as jnp
from jax import lax
from jax.experimental import pallas as pl
from jax.experimental.pallas import tpu as pltpu
from jax.sharding import PartitionSpec as P

MESH = pl.DeviceIdType.MESH
F32 = jnp.float32
BF16 = jnp.bfloat16
SMOOTHING = 0.01
INVERSE_FOUR_PI = 1.0 / (4.0 * math.pi)

LEAVES = 64
POINTS = 256
RANK = 64
NEAR = 8
FAR = 16
TERMS = 32
PAIRS = LEAVES * NEAR
GROUP = 8
CHUNK = 8
DEVICES = 128
BLOCK = 8
BLOCKS = DEVICES // BLOCK
BLANK = 3 * LEAVES


def split3(value):
    high = value.astype(BF16).astype(F32)
    rest = value - high
    middle = rest.astype(BF16).astype(F32)
    low = (rest - middle).astype(BF16).astype(F32)
    return high, middle, low


def centred(points):
    shifted = [p - 1.0 for p in points]
    norm = shifted[0] * shifted[0] + shifted[1] * shifted[1] + shifted[2] * shifted[2]
    return [split3(u) for u in shifted], norm


def source_terms(parts, norm):
    rows = []
    for high, middle, low in parts:
        high, middle, low = -2.0 * high, -2.0 * middle, -2.0 * low
        rows += [high, high, high, middle, middle, low]
    one = jnp.ones_like(norm)
    return rows + list(split3(norm + SMOOTHING)) + [one, one, one]


def target_terms(parts, norm):
    rows = []
    for high, middle, low in parts:
        rows += [high, middle, low, high, middle, high]
    one = jnp.ones_like(norm)
    return rows + [one, one, one] + list(split3(norm))


def by_leaf(rows):
    blank = jnp.zeros_like(rows[0])
    return jnp.swapaxes(jnp.stack(rows + [blank] * (TERMS - len(rows)), axis=0), 0, 1)


def eye():
    shape = (RANK, RANK)
    return (lax.broadcasted_iota(jnp.int32, shape, 0) == lax.broadcasted_iota(jnp.int32, shape, 1)).astype(F32)


def to_column(row, unit):
    return jnp.sum(unit * row, axis=1, keepdims=True)


def to_row(column, unit):
    return jnp.sum(unit * column, axis=0, keepdims=True)


def exchange_kernel(
    charges, points, near, far, cluster_transfer, bases_hbm, transfer_hbm,
    source_out, target_out, charge_out, moment_out, every_out, far_out, pair_out,
    bases, transfer, halo_charges, halo_points, window, every,
    load_sems, halo_send, halo_recv, moment_send, moment_recv, one_send, one_recv, two_send, two_recv,
):
    gx, gy = lax.axis_index("gx"), lax.axis_index("gy")
    device = gx * 4 + gy

    def place(index):
        return (index // 4, index % 4)

    def beside(distance):
        return place((device + distance + DEVICES) % DEVICES)

    place_in_block = device % BLOCK
    block = device // BLOCK
    chunks = LEAVES // CHUNK

    def load_copies(c):
        span = pl.ds(c * CHUNK, CHUNK)
        return (
            pltpu.make_async_copy(bases_hbm.at[span], bases.at[span], load_sems.at[0, c]),
            pltpu.make_async_copy(transfer_hbm.at[span], transfer.at[span], load_sems.at[1, c]),
        )

    @pl.loop(0, chunks)
    def _(c):
        for copy in load_copies(c):
            copy.start()

    barrier = pltpu.get_barrier_semaphore()
    for distance in (1, -1, 2, -2):
        pl.semaphore_signal(barrier, inc=1, device_id=beside(distance), device_id_type=MESH)

    def block_mate(k):
        return place(block * BLOCK + (place_in_block + k) % BLOCK)

    def far_mate(k):
        return place(((block + k) % BLOCKS) * BLOCK + place_in_block)

    @pl.loop(1, BLOCK)
    def _(k):
        pl.semaphore_signal(barrier, inc=1, device_id=block_mate(k), device_id_type=MESH)

    @pl.loop(1, BLOCKS)
    def _(k):
        pl.semaphore_signal(barrier, inc=1, device_id=far_mate(k), device_id_type=MESH)

    pl.semaphore_wait(barrier, 4 + BLOCK - 1 + BLOCKS - 1)

    def halo_copies():
        copies = []
        for side, distance in ((0, 1), (1, -1)):
            for kind, (source, landing) in enumerate(((charges, halo_charges), (points, halo_points))):
                copies.append(
                    pltpu.make_async_remote_copy(
                        src_ref=source,
                        dst_ref=landing.at[side],
                        send_sem=halo_send.at[side, kind],
                        recv_sem=halo_recv.at[side, kind],
                        device_id=beside(distance),
                        device_id_type=MESH,
                    )
                )
        return copies

    halo = halo_copies()
    for copy in halo:
        copy.start()

    lane = lax.broadcasted_iota(jnp.int32, (RANK, LEAVES), 1)

    def moment_chunk(c, carry):
        columns, total = carry
        for copy in load_copies(c):
            copy.wait()
        weights = charges[pl.ds(pl.multiple_of(c * CHUNK, CHUNK), CHUNK), :]
        for k in range(CHUNK):
            product = bases[c * CHUNK + k] * weights[k : k + 1, :]
            column = jnp.sum(product[:, :128] + product[:, 128:], axis=1, keepdims=True)
            columns = jnp.where(lane == c * CHUNK + k, column, columns)
            total = total + transfer[c * CHUNK + k] * column
        return columns, total

    columns, total = lax.fori_loop(
        0, chunks, moment_chunk, (jnp.zeros((RANK, LEAVES), F32), jnp.zeros((RANK, RANK), F32))
    )
    window[2] = columns.T
    unit = eye()
    cluster_row = jnp.sum(total, axis=0, keepdims=True)
    lifted_row = jnp.sum(cluster_transfer[0] * to_column(cluster_row, unit), axis=0, keepdims=True)
    every[device, 0:1, 0:RANK] = cluster_row
    every[device, 0:1, RANK : 2 * RANK] = lifted_row

    def one_copy(k):
        return pltpu.make_async_remote_copy(
            src_ref=every.at[device],
            dst_ref=every.at[device],
            send_sem=one_send.at[k],
            recv_sem=one_recv.at[k],
            device_id=block_mate(k),
            device_id_type=MESH,
        )

    def two_copy(k):
        rows = pl.ds(block * BLOCK, BLOCK)
        return pltpu.make_async_remote_copy(
            src_ref=every.at[rows],
            dst_ref=every.at[rows],
            send_sem=two_send.at[k],
            recv_sem=two_recv.at[k],
            device_id=far_mate(k),
            device_id_type=MESH,
        )

    @pl.loop(1, BLOCK)
    def _(k):
        one_copy(k).start()

    def moment_copies():
        copies = []
        for n, distance in enumerate((2, 1, -1, -2)):
            slot = (0, 1, 3, 4)[n]
            copies.append(
                pltpu.make_async_remote_copy(
                    src_ref=window.at[2],
                    dst_ref=window.at[slot],
                    send_sem=moment_send.at[n],
                    recv_sem=moment_recv.at[n],
                    device_id=beside(distance),
                    device_id_type=MESH,
                )
            )
        return copies

    moments = moment_copies()
    for copy in moments:
        copy.start()

    @pl.loop(0, chunks)
    def _(c):
        span = pl.ds(pl.multiple_of(c * CHUNK, CHUNK), CHUNK)
        parts, norm = centred([points[n, span, :] for n in range(3)])
        source_out[pl.ds(LEAVES + c * CHUNK, CHUNK)] = by_leaf(source_terms(parts, norm)).astype(BF16)
        target = by_leaf(target_terms(parts, norm))
        for k in range(CHUNK):
            target_out[c * CHUNK + k] = target[k].T.astype(BF16)

    charge_out[LEAVES : 2 * LEAVES] = charges[...]
    charge_out[3 * LEAVES :] = jnp.zeros((8, POINTS), F32)
    term = lax.broadcasted_iota(jnp.int32, (TERMS, POINTS), 0)
    source_out[BLANK] = jnp.where(term == 18, 1.0, 0.0).astype(BF16)

    far_targets = far[...]
    far_out[...] = jnp.where(far_targets >= 0, far_targets - (device - 2) * LEAVES, 5 * LEAVES)

    slots = near[...]
    live = (slots >= 0).astype(F32)
    before = (
        lax.broadcasted_iota(jnp.int32, (LEAVES, LEAVES), 0) < lax.broadcasted_iota(jnp.int32, (LEAVES, LEAVES), 1)
    ).astype(BF16)
    rank_in_slot = jnp.dot(live.astype(BF16), before, preferred_element_type=F32)
    in_slot = jnp.sum(live, axis=1, keepdims=True)
    leaf_row = lax.broadcasted_iota(jnp.int32, (1, LEAVES), 1)
    code = (leaf_row * 256 + slots - (device - 1) * LEAVES).astype(F32)
    position_row = lax.broadcasted_iota(jnp.int32, (1, PAIRS), 1).astype(F32)
    found = jnp.zeros((LEAVES, PAIRS), F32)
    start = jnp.zeros((1, 1), F32)
    positions = []
    for s in range(NEAR):
        positions.append(jnp.where(live[s : s + 1] > 0, rank_in_slot[s : s + 1] + start, -1.0))
        start = start + in_slot[s : s + 1]
    table = jnp.concatenate(positions + [code], axis=0).T
    for s in range(NEAR):
        found = jnp.where(table[:, s : s + 1] == position_row, table[:, NEAR + s : NEAR + s + 1], found)
    pairs = jnp.sum(found, axis=0, keepdims=True)
    pair_out[0:1] = jnp.where(position_row < start, pairs, float(BLANK)).astype(jnp.int32)
    far_live = jnp.sum((far_targets >= 0).astype(F32), axis=0, keepdims=True).astype(jnp.int32)
    pair_out[1:2] = jnp.concatenate(
        [far_live, jnp.broadcast_to(start.astype(jnp.int32), (1, PAIRS - LEAVES))], axis=1
    )

    @pl.loop(1, BLOCK)
    def _(k):
        one_copy(k).wait_recv()

    @pl.loop(1, BLOCKS)
    def _(k):
        two_copy(k).start()

    for side in range(2):
        halo[2 * side].wait_recv()
        halo[2 * side + 1].wait_recv()
        first = 2 * LEAVES * side

        @pl.loop(0, chunks)
        def _(c):
            span = pl.ds(pl.multiple_of(c * CHUNK, CHUNK), CHUNK)
            parts, norm = centred([halo_points[side, n, span, :] for n in range(3)])
            source_out[pl.ds(first + c * CHUNK, CHUNK)] = by_leaf(source_terms(parts, norm)).astype(BF16)

        charge_out[first : first + LEAVES] = halo_charges[side]

    for copy in moments:
        copy.wait_recv()
    for n in range(5):
        moment_out[n * LEAVES : (n + 1) * LEAVES] = window[n]
    moment_out[5 * LEAVES :] = jnp.zeros((8, RANK), F32)

    @pl.loop(1, BLOCKS)
    def _(k):
        two_copy(k).wait_recv()

    every_out[...] = every[...]

    @pl.loop(1, BLOCK)
    def _(k):
        one_copy(k).wait_send()

    @pl.loop(1, BLOCKS)
    def _(k):
        two_copy(k).wait_send()

    for copy in halo + moments:
        copy.wait_send()


def local_kernel(
    pairs, far, cluster_target, group_target, top_target,
    source, target, charges, moments, every,
    cluster_transfer, cluster_coupling, group_coupling,
    bases_hbm, transfer_hbm, group_transfer_hbm, top_coupling_hbm, coupling_hbm,
    out,
    near_total, coupling, bases, transfer, group_transfer, top_coupling, group_moments, top_moments,
    coupling_sems, sems,
):
    gx = lax.axis_index("gx")
    top = gx // 4

    def coupling_copy(i):
        count = pairs[1, i]
        return pltpu.make_async_copy(
            coupling_hbm.at[i, pl.ds(0, count)], coupling.at[i, pl.ds(0, count)], coupling_sems.at[i]
        )

    loads = [
        pltpu.make_async_copy(group_transfer_hbm, group_transfer, sems.at[0]),
        pltpu.make_async_copy(top_coupling_hbm.at[top], top_coupling, sems.at[1]),
        pltpu.make_async_copy(transfer_hbm, transfer, sems.at[2]),
        pltpu.make_async_copy(bases_hbm, bases, sems.at[3]),
    ]
    for copy in loads:
        copy.start()

    @pl.loop(0, LEAVES)
    def _(i):
        @pl.when(pairs[1, i] > 0)
        def _():
            coupling_copy(i).start()

    @pl.loop(0, LEAVES)
    def _(i):
        near_total[i] = jnp.zeros((POINTS, 128), F32)

    @pl.loop(0, (pairs[1, LEAVES] + GROUP - 1) // GROUP)
    def _(g):
        for k in range(GROUP):
            code = pairs[0, g * GROUP + k]
            i, j = code // 256, code % 256
            distance = jnp.dot(target[i], source[j], preferred_element_type=F32)
            weighted = lax.rsqrt(distance) * charges[pl.ds(j, 1), :]
            near_total[i] += weighted[:, :128] + weighted[:, 128:]

    unit = eye()
    for copy in loads:
        copy.wait()

    for g in range(32):
        group_moments[g : g + 1] = (
            every[4 * g, :, RANK:] + every[4 * g + 1, :, RANK:] + every[4 * g + 2, :, RANK:] + every[4 * g + 3, :, RANK:]
        )
    for h in range(8):
        total = jnp.zeros((RANK, RANK), F32)
        for k in range(4):
            g = 4 * h + k
            total = total + group_transfer[g] * to_column(group_moments[g : g + 1], unit)
        top_moments[h : h + 1] = jnp.sum(total, axis=0, keepdims=True)

    def masked(t):
        return jnp.where(t >= 0, 1.0, 0.0).astype(F32), jnp.maximum(t, 0)

    total = jnp.zeros((RANK, RANK), F32)
    for f in range(4):
        weight, t = masked(top_target[top, f])
        total = total + top_coupling[f] * (top_moments[pl.ds(t, 1), :] * weight)
    top_local = to_row(jnp.sum(total, axis=1, keepdims=True), unit)
    total = group_transfer[gx] * top_local
    for f in range(8):
        weight, t = masked(group_target[0, f])
        total = total + group_coupling[0, f] * (group_moments[pl.ds(t, 1), :] * weight)
    group_local = to_row(jnp.sum(total, axis=1, keepdims=True), unit)
    total = cluster_transfer[0] * group_local
    for f in range(8):
        weight, t = masked(cluster_target[0, f])
        total = total + cluster_coupling[0, f] * (every[t, :, :RANK] * weight)
    cluster_local = to_row(jnp.sum(total, axis=1, keepdims=True), unit)

    @pl.loop(0, LEAVES // 2)
    def _(step):
        for k in range(2):
            i = step * 2 + k

            @pl.when(pairs[1, i] > 0)
            def _():
                coupling_copy(i).wait()

            total = transfer[i] * cluster_local
            total = lax.fori_loop(
                0, pairs[1, i], lambda f, total: total + coupling[i, f] * moments[pl.ds(far[f, i], 1), :], total
            )
            leaf_local = jnp.sum(total, axis=1, keepdims=True)
            far_part = jnp.sum(bases[i] * leaf_local, axis=0, keepdims=True)
            near_part = jnp.sum(near_total[i].T, axis=0, keepdims=True)
            out[pl.ds(i, 1), :] = near_part * INVERSE_FOUR_PI + far_part


def local(
    charges, points, leaf_bases, leaf_transfer, near_target, far_target, leaf_coupling, cluster_transfer,
    cluster_target, cluster_coupling, group_transfer, group_target, group_coupling, top_target, top_coupling,
):
    vmem = pl.BlockSpec(memory_space=pltpu.VMEM)
    smem = pl.BlockSpec(memory_space=pltpu.SMEM)
    anywhere = pl.BlockSpec(memory_space=pl.ANY)
    dma = pltpu.SemaphoreType.DMA
    bases = jnp.swapaxes(leaf_bases, 1, 2)
    source, target, all_charges, moments, every, far, pairs = pl.pallas_call(
        exchange_kernel,
        out_shape=(
            jax.ShapeDtypeStruct((3 * LEAVES + 1, TERMS, POINTS), BF16),
            jax.ShapeDtypeStruct((LEAVES, POINTS, TERMS), BF16),
            jax.ShapeDtypeStruct((3 * LEAVES + 8, POINTS), F32),
            jax.ShapeDtypeStruct((5 * LEAVES + 8, RANK), F32),
            jax.ShapeDtypeStruct((DEVICES, 1, 2 * RANK), F32),
            jax.ShapeDtypeStruct((FAR, LEAVES), jnp.int32),
            jax.ShapeDtypeStruct((2, PAIRS), jnp.int32),
        ),
        in_specs=[vmem] * 5 + [anywhere] * 2,
        out_specs=[vmem] * 7,
        scratch_shapes=[
            pltpu.VMEM((LEAVES, RANK, POINTS), F32),
            pltpu.VMEM((LEAVES, RANK, RANK), F32),
            pltpu.VMEM((2, LEAVES, POINTS), F32),
            pltpu.VMEM((2, 3, LEAVES, POINTS), F32),
            pltpu.VMEM((5, LEAVES, RANK), F32),
            pltpu.VMEM((DEVICES, 1, 2 * RANK), F32),
            dma((2, LEAVES // CHUNK)),
            dma((2, 2)),
            dma((2, 2)),
            dma((4,)),
            dma((4,)),
            dma((BLOCK,)),
            dma((BLOCK,)),
            dma((BLOCKS,)),
            dma((BLOCKS,)),
        ],
        compiler_params=pltpu.CompilerParams(
            collective_id=0, has_side_effects=True, vmem_limit_bytes=48 << 20
        ),
        name="exchange",
    )(
        charges,
        jnp.transpose(points, (1, 0, 2)),
        near_target.T,
        far_target.T,
        cluster_transfer,
        bases,
        leaf_transfer,
    )
    return pl.pallas_call(
        local_kernel,
        out_shape=jax.ShapeDtypeStruct((LEAVES, POINTS), F32),
        in_specs=[smem] * 5 + [vmem] * 8 + [anywhere] * 5,
        out_specs=vmem,
        scratch_shapes=[
            pltpu.VMEM((LEAVES, POINTS, 128), F32),
            pltpu.VMEM((LEAVES, FAR, RANK, RANK), F32),
            pltpu.VMEM((LEAVES, RANK, POINTS), F32),
            pltpu.VMEM((LEAVES, RANK, RANK), F32),
            pltpu.VMEM((32, RANK, RANK), F32),
            pltpu.VMEM((4, RANK, RANK), F32),
            pltpu.VMEM((32, RANK), F32),
            pltpu.VMEM((8, RANK), F32),
            dma((LEAVES,)),
            dma((4,)),
        ],
        compiler_params=pltpu.CompilerParams(vmem_limit_bytes=62 << 20),
        name="local",
    )(
        pairs, far, cluster_target, group_target, top_target,
        source, target, all_charges, moments, every,
        cluster_transfer, cluster_coupling, group_coupling,
        bases, leaf_transfer, group_transfer, top_coupling, leaf_coupling,
    )


def solution(mesh):
    leaf = ("gx", "gy")
    return jax.shard_map(
        local,
        mesh=mesh,
        in_specs=(
            P(leaf, None),
            P(leaf, None, None),
            P(leaf, None, None),
            P(leaf, None, None),
            P(leaf, None),
            P(leaf, None),
            P(leaf, None, None, None),
            P(leaf, None, None),
            P(leaf, None),
            P(leaf, None, None, None),
            P(),
            P("gx", None),
            P("gx", None, None, None),
            P(),
            P(),
        ),
        out_specs=P(leaf, None),
        check_vma=False,
    )
```

profile of v0, /device:TPU:1, one launch (start us, length us, event | category | flops | bytes accessed | tf_op | source)
XLA Modules:
  0.0 76.6 jit_solution(5682835792915190729)
XLA Ops:
  0.0 1.3 %copy.16.top_target = s32[8,4]{1,0:T(8,128)} copy(s32[8,4]{0,1:T(4,128)} %param.28) | data formatting | bytes 256 | tf_op args[13]
  1.3 0.0 copy-start
  1.4 1.6 %copy-done = f32[64,64,64]{2,1,0:T(8,128)S(1)} copy-done((f32[64,64,64]{2,1,0:T(8,128)S(1)}, f32[64,64,64]{2,1,0:T(8,128)}, u32[]{:S(2)}) %copy-start) | copy-done | bytes 1048600
  2.9 0.0 copy-start.3
  2.9 0.9 %copy-done.3 = f32[64,3,256]{2,0,1:T(8,128)S(1)} copy-done((f32[64,3,256]{2,0,1:T(8,128)S(1)}, f32[64,3,256]{2,0,1:T(8,128)}, u32[]{:S(2)}) %copy-start.3) | copy-done | bytes 196632
  3.9 0.0 copy-start.5
  3.9 0.8 copy-done.5
  4.6 0.0 copy-start.6
  4.6 0.8 %copy-done.6 = f32[64,256]{1,0:T(8,128)S(1)} copy-done((f32[64,256]{1,0:T(8,128)S(1)}, f32[64,256]{1,0:T(8,128)}, u32[]{:S(2)}) %copy-start.6) | copy-done | bytes 65560
  5.5 0.0 copy-start.8
  5.5 0.7 copy-done.8
  6.2 0.0 copy-start.11
  6.2 0.7 copy-done.11
  6.9 25.6 %exchange.1 = (bf16[193,32,256]{2,1,0:T(8,128)(2,1)S(1)}, bf16[64,256,32]{2,1,0:T(8,128)(2,1)}, f32[200,256]{1,0:T(8,128)S(1)}, f32[328,64]{1,0:T(8,128)S(1)}, f...) custom-call(f32[64,256]{1,0:T(8,128)S(1)} %copy-done.6, f32[3,64,256]{2,1,0:T(8,128)S(1)} %bitcast.4, ...), custom_call_target="tpu_custom_call" | custom-call | tf_op jit(solution)/shard_map/exchange/pallas_call | solution.py:417
  32.4 0.0 copy-start.1
  32.5 1.7 %copy-done.1 = bf16[193,32,256]{2,1,0:T(8,128)(2,1)} copy-done((bf16[193,32,256]{2,1,0:T(8,128)(2,1)}, bf16[193,32,256]{2,1,0:T(8,128)(2,1)S(1)}, u32[]{:S(2)}) %copy-start.1) | copy-done | bytes 3162136
  34.1 0.0 copy-start.2
  34.1 0.7 copy-done.2
  34.8 0.0 copy-start.4
  34.8 0.7 copy-done.4
  35.5 0.0 copy-start.7
  35.5 0.6 copy-done.7
  36.1 0.0 copy-start.9
  36.1 0.6 copy-done.9
  36.7 0.0 copy-start.10
  36.7 0.6 copy-done.10
  37.3 39.3 %local.1 = f32[64,256]{1,0:T(8,128)} custom-call(s32[2,512]{1,0:T(2,128)} %copy-done.10, s32[16,64]{1,0:T(8,128)} %copy-done.9, s32[1,8]{1,0:T(1,128)} %cluster_target.1, s32[1,8]{1,0:T(1,128)} %group_target.1, s32[8,4]{1,0:T(8,128)} %copy.16.top_target, bf16[193,32,256]{2,1,0:T(8,128)(2,1)} %copy-done.1, bf16[64,256,32]{2,1,0:T(8,128)(2,1)} %get-tuple-element.15.target, ...), custom_call_target="tpu_custom_call" | custom-call | tf_op jit(solution)/shard_map/local/pallas_call | solution.py:460
Async XLA Ops:
  1.3 1.6 %copy-start = (f32[64,64,64]{2,1,0:T(8,128)S(1)}, f32[64,64,64]{2,1,0:T(8,128)}, u32[]{:S(2)}) copy-start(f32[64,64,64]{2,1,0:T(8,128)} %transfer_hbm.3) | copy-start | bytes 3145732
  2.9 0.9 %copy-start.3 = (f32[64,3,256]{2,0,1:T(8,128)S(1)}, f32[64,3,256]{2,0,1:T(8,128)}, u32[]{:S(2)}) copy-start(f32[64,3,256]{2,0,1:T(8,128)} %param.16) | copy-start | bytes 589828
  3.9 0.8 copy-start.5
  4.6 0.8 %copy-start.6 = (f32[64,256]{1,0:T(8,128)S(1)}, f32[64,256]{1,0:T(8,128)}, u32[]{:S(2)}) copy-start(f32[64,256]{1,0:T(8,128)} %charges.1) | copy-start | bytes 196612
  5.5 0.7 copy-start.8
  6.2 0.7 copy-start.11
  32.4 1.7 %copy-start.1 = (bf16[193,32,256]{2,1,0:T(8,128)(2,1)}, bf16[193,32,256]{2,1,0:T(8,128)(2,1)S(1)}, u32[]{:S(2)}) copy-start(bf16[193,32,256]{2,1,0:T(8,128)(2,1)S(1)} %get-tuple-element.14.source) | copy-start | bytes 9486340
  34.1 0.7 copy-start.2
  34.8 0.7 copy-start.4
  35.5 0.6 copy-start.7
  36.1 0.6 copy-start.9
  36.7 0.6 copy-start.10
where the time goes:
time: 77.5 us; the launch traced here: 76.6 us
  Pallas kernels  64.9 us (84%)
  local copies, waits for them, and re-layouts  11.6 us (15%)
    pallas_call x1, Pallas kernels, local(): pl.pallas_call(local_kernel, out_shape=jax.ShapeDtypeStruct((LEAVES, POIN...  39.3 us
    pallas_call x1, Pallas kernels, local(): pl.pallas_call(exchange_kernel, out_shape=(jax.ShapeDtypeStruct((3 * LEAV...  25.6 us
    unnamed x25, local copies, waits for them, and re-layouts  11.6 us

commit v1 on v0

--- a/solution.py
+++ b/solution.py
@@ -23,6 +23,7 @@
 PAIRS = LEAVES * NEAR
 GROUP = 8
 CHUNK = 8
+FAR_LEAVES = 2
 DEVICES = 128
 BLOCK = 8
 BLOCKS = DEVICES // BLOCK
@@ -79,10 +80,10 @@
 
 
 def exchange_kernel(
-    charges, points, near, far, cluster_transfer, bases_hbm, transfer_hbm,
-    source_out, target_out, charge_out, moment_out, every_out, far_out, pair_out,
-    bases, transfer, halo_charges, halo_points, window, every,
-    load_sems, halo_send, halo_recv, moment_send, moment_recv, one_send, one_recv, two_send, two_recv,
+    charges_hbm, points_hbm, near_hbm, far_hbm, cluster_transfer_hbm, bases_hbm, transfer_hbm,
+    source_out, target_out, charge_out, moment_out, every_out, far_out, pair_out, bases, transfer,
+    charges, points, near, far, cluster_transfer, halo_charges, halo_points, window, every,
+    load_sems, small_sems, halo_send, halo_recv, moment_send, moment_recv, one_send, one_recv, two_send, two_recv,
 ):
     gx, gy = lax.axis_index("gx"), lax.axis_index("gy")
     device = gx * 4 + gy
@@ -104,6 +105,21 @@
             pltpu.make_async_copy(transfer_hbm.at[span], transfer.at[span], load_sems.at[1, c]),
         )
 
+    small = [
+        pltpu.make_async_copy(source, landing, small_sems.at[n])
+        for n, (source, landing) in enumerate(
+            (
+                (charges_hbm, charges),
+                (points_hbm, points),
+                (near_hbm, near),
+                (far_hbm, far),
+                (cluster_transfer_hbm, cluster_transfer),
+            )
+        )
+    ]
+    for copy in small:
+        copy.start()
+
     @pl.loop(0, chunks)
     def _(c):
         for copy in load_copies(c):
@@ -127,6 +143,8 @@
     def _(k):
         pl.semaphore_signal(barrier, inc=1, device_id=far_mate(k), device_id_type=MESH)
 
+    for copy in small:
+        copy.wait()
     pl.semaphore_wait(barrier, 4 + BLOCK - 1 + BLOCKS - 1)
 
     def halo_copies():
@@ -255,9 +273,10 @@
     for s in range(NEAR):
         found = jnp.where(table[:, s : s + 1] == position_row, table[:, NEAR + s : NEAR + s + 1], found)
     pairs = jnp.sum(found, axis=0, keepdims=True)
-    pair_out[0:1] = jnp.where(position_row < start, pairs, float(BLANK)).astype(jnp.int32)
+    pair_out[0:1, 0:PAIRS] = jnp.where(position_row < start, pairs, float(BLANK)).astype(jnp.int32)
+    pair_out[0:1, PAIRS:] = jnp.full((1, 128), BLANK, jnp.int32)
     far_live = jnp.sum((far_targets >= 0).astype(F32), axis=0, keepdims=True).astype(jnp.int32)
-    pair_out[1:2] = jnp.concatenate(
+    pair_out[1:2, 0:PAIRS] = jnp.concatenate(
         [far_live, jnp.broadcast_to(start.astype(jnp.int32), (1, PAIRS - LEAVES))], axis=1
     )
 
@@ -307,53 +326,97 @@
 
 
 def local_kernel(
-    pairs, far, cluster_target, group_target, top_target,
-    source, target, charges, moments, every,
-    cluster_transfer, cluster_coupling, group_coupling,
-    bases_hbm, transfer_hbm, group_transfer_hbm, top_coupling_hbm, coupling_hbm,
+    source, target, charges, moments, every, far_vmem, pairs_vmem, bases, transfer,
+    cluster_target_hbm, group_target_hbm, top_target_hbm, cluster_transfer_hbm, cluster_coupling_hbm,
+    group_coupling_hbm, group_transfer_hbm, top_coupling_hbm, coupling_hbm,
     out,
-    near_total, coupling, bases, transfer, group_transfer, top_coupling, group_moments, top_moments,
+    near_total, ahead, coupling, cluster_transfer, cluster_coupling, group_coupling, group_transfer, top_coupling,
+    group_moments, top_moments, pairs, far, cluster_target, group_target, top_target,
     coupling_sems, sems,
 ):
     gx = lax.axis_index("gx")
     top = gx // 4
 
-    def coupling_copy(i):
-        count = pairs[1, i]
-        return pltpu.make_async_copy(
-            coupling_hbm.at[i, pl.ds(0, count)], coupling.at[i, pl.ds(0, count)], coupling_sems.at[i]
-        )
-
     loads = [
-        pltpu.make_async_copy(group_transfer_hbm, group_transfer, sems.at[0]),
-        pltpu.make_async_copy(top_coupling_hbm.at[top], top_coupling, sems.at[1]),
-        pltpu.make_async_copy(transfer_hbm, transfer, sems.at[2]),
-        pltpu.make_async_copy(bases_hbm, bases, sems.at[3]),
+        pltpu.make_async_copy(source_ref, landing, sems.at[n])
+        for n, (source_ref, landing) in enumerate(
+            (
+                (pairs_vmem, pairs),
+                (far_vmem, far),
+                (cluster_target_hbm, cluster_target),
+                (group_target_hbm, group_target),
+                (top_target_hbm, top_target),
+                (cluster_transfer_hbm, cluster_transfer),
+                (cluster_coupling_hbm, cluster_coupling),
+                (group_coupling_hbm, group_coupling),
+                (group_transfer_hbm, group_transfer),
+                (top_coupling_hbm.at[top], top_coupling),
+            )
+        )
     ]
     for copy in loads:
         copy.start()
 
+    @pl.loop(0, LEAVES // 4)
+    def _(c):
+        for k in range(4):
+            near_total[c * 4 + k] = jnp.zeros((POINTS, 128), F32)
+
+    coupling[LEAVES * FAR] = jnp.zeros((RANK, RANK), F32)
+    for copy in loads[:2]:
+        copy.wait()
+
+    def coupling_copy(i):
+        count = jnp.maximum(pairs[1, i], 1)
+        return pltpu.make_async_copy(
+            coupling_hbm.at[pl.ds(i * FAR, count)], coupling.at[pl.ds(i * FAR, count)], coupling_sems.at[i]
+        )
+
     @pl.loop(0, LEAVES)
     def _(i):
-        @pl.when(pairs[1, i] > 0)
-        def _():
-            coupling_copy(i).start()
-
-    @pl.loop(0, LEAVES)
-    def _(i):
-        near_total[i] = jnp.zeros((POINTS, 128), F32)
-
-    @pl.loop(0, (pairs[1, LEAVES] + GROUP - 1) // GROUP)
+        coupling_copy(i).start()
+
+    def squares(p):
+        code = pairs[0, p]
+        return jnp.dot(target[code // 256], source[code % 256], preferred_element_type=F32)
+
+    def add_near(p, square):
+        code = pairs[0, p]
+        weighted = lax.rsqrt(square) * charges[pl.ds(code % 256, 1), :]
+        near_total[code // 256] += weighted[:, :128] + weighted[:, 128:]
+
+    def near_group(g):
+        add_near(g * GROUP, ahead[...])
+        for k in range(1, GROUP):
+            add_near(g * GROUP + k, squares(g * GROUP + k))
+        ahead[...] = squares(g * GROUP + GROUP)
+
+    def far_leaf(i):
+        count = pairs[1, i]
+        total = None
+        for f in range(FAR):
+            index = jnp.where(f < count, i * FAR + f, LEAVES * FAR)
+            term = coupling[index] * moments[pl.ds(far[f, i], 1), :]
+            total = term if total is None else total + term
+        coupling[i * FAR] = total
+
+    ahead[...] = squares(0)
+    shared = LEAVES // FAR_LEAVES
+
+    @pl.loop(0, shared)
     def _(g):
-        for k in range(GROUP):
-            code = pairs[0, g * GROUP + k]
-            i, j = code // 256, code % 256
-            distance = jnp.dot(target[i], source[j], preferred_element_type=F32)
-            weighted = lax.rsqrt(distance) * charges[pl.ds(j, 1), :]
-            near_total[i] += weighted[:, :128] + weighted[:, 128:]
+        for k in range(FAR_LEAVES):
+            coupling_copy(g * FAR_LEAVES + k).wait()
+        for k in range(FAR_LEAVES):
+            far_leaf(g * FAR_LEAVES + k)
+        near_group(g)
+
+    @pl.loop(shared, jnp.maximum((pairs[1, LEAVES] + GROUP - 1) // GROUP, shared))
+    def _(g):
+        near_group(g)
 
     unit = eye()
-    for copy in loads:
+    for copy in loads[2:]:
         copy.wait()
 
     for g in range(32):
@@ -372,7 +435,7 @@
 
     total = jnp.zeros((RANK, RANK), F32)
     for f in range(4):
-        weight, t = masked(top_target[top, f])
+        weight, t = masked(top_target[f, top])
         total = total + top_coupling[f] * (top_moments[pl.ds(t, 1), :] * weight)
     top_local = to_row(jnp.sum(total, axis=1, keepdims=True), unit)
     total = group_transfer[gx] * top_local
@@ -386,23 +449,17 @@
         total = total + cluster_coupling[0, f] * (every[t, :, :RANK] * weight)
     cluster_local = to_row(jnp.sum(total, axis=1, keepdims=True), unit)
 
-    @pl.loop(0, LEAVES // 2)
-    def _(step):
-        for k in range(2):
-            i = step * 2 + k
-
-            @pl.when(pairs[1, i] > 0)
-            def _():
-                coupling_copy(i).wait()
-
-            total = transfer[i] * cluster_local
-            total = lax.fori_loop(
-                0, pairs[1, i], lambda f, total: total + coupling[i, f] * moments[pl.ds(far[f, i], 1), :], total
-            )
+    @pl.loop(0, LEAVES // CHUNK)
+    def _(c):
+        rows = []
+        for k in range(CHUNK):
+            i = c * CHUNK + k
+            total = transfer[i] * cluster_local + coupling[i * FAR]
             leaf_local = jnp.sum(total, axis=1, keepdims=True)
             far_part = jnp.sum(bases[i] * leaf_local, axis=0, keepdims=True)
             near_part = jnp.sum(near_total[i].T, axis=0, keepdims=True)
-            out[pl.ds(i, 1), :] = near_part * INVERSE_FOUR_PI + far_part
+            rows.append(near_part * INVERSE_FOUR_PI + far_part)
+        out[pl.ds(pl.multiple_of(c * CHUNK, CHUNK), CHUNK), :] = jnp.concatenate(rows, axis=0)
 
 
 def local(
@@ -410,31 +467,39 @@
     cluster_target, cluster_coupling, group_transfer, group_target, group_coupling, top_target, top_coupling,
 ):
     vmem = pl.BlockSpec(memory_space=pltpu.VMEM)
-    smem = pl.BlockSpec(memory_space=pltpu.SMEM)
     anywhere = pl.BlockSpec(memory_space=pl.ANY)
     dma = pltpu.SemaphoreType.DMA
-    bases = jnp.swapaxes(leaf_bases, 1, 2)
-    source, target, all_charges, moments, every, far, pairs = pl.pallas_call(
+
+    def in_hbm(*arrays):
+        return [pltpu.with_memory_space_constraint(array, pltpu.HBM) for array in arrays]
+
+    handed = pl.pallas_call(
         exchange_kernel,
         out_shape=(
-            jax.ShapeDtypeStruct((3 * LEAVES + 1, TERMS, POINTS), BF16),
-            jax.ShapeDtypeStruct((LEAVES, POINTS, TERMS), BF16),
-            jax.ShapeDtypeStruct((3 * LEAVES + 8, POINTS), F32),
-            jax.ShapeDtypeStruct((5 * LEAVES + 8, RANK), F32),
-            jax.ShapeDtypeStruct((DEVICES, 1, 2 * RANK), F32),
-            jax.ShapeDtypeStruct((FAR, LEAVES), jnp.int32),
-            jax.ShapeDtypeStruct((2, PAIRS), jnp.int32),
-        ),
-        in_specs=[vmem] * 5 + [anywhere] * 2,
-        out_specs=[vmem] * 7,
-        scratch_shapes=[
+            pltpu.VMEM((3 * LEAVES + 1, TERMS, POINTS), BF16),
+            pltpu.VMEM((LEAVES, POINTS, TERMS), BF16),
+            pltpu.VMEM((3 * LEAVES + 8, POINTS), F32),
+            pltpu.VMEM((5 * LEAVES + 8, RANK), F32),
+            pltpu.VMEM((DEVICES, 1, 2 * RANK), F32),
+            pltpu.VMEM((FAR, LEAVES), jnp.int32),
+            pltpu.VMEM((2, PAIRS + 128), jnp.int32),
             pltpu.VMEM((LEAVES, RANK, POINTS), F32),
             pltpu.VMEM((LEAVES, RANK, RANK), F32),
+        ),
+        in_specs=[anywhere] * 7,
+        out_specs=[vmem] * 9,
+        scratch_shapes=[
+            pltpu.VMEM((LEAVES, POINTS), F32),
+            pltpu.VMEM((3, LEAVES, POINTS), F32),
+            pltpu.VMEM((NEAR, LEAVES), jnp.int32),
+            pltpu.VMEM((FAR, LEAVES), jnp.int32),
+            pltpu.VMEM((1, RANK, RANK), F32),
             pltpu.VMEM((2, LEAVES, POINTS), F32),
             pltpu.VMEM((2, 3, LEAVES, POINTS), F32),
             pltpu.VMEM((5, LEAVES, RANK), F32),
             pltpu.VMEM((DEVICES, 1, 2 * RANK), F32),
             dma((2, LEAVES // CHUNK)),
+            dma((5,)),
             dma((2, 2)),
             dma((2, 2)),
             dma((4,)),
@@ -445,42 +510,59 @@
             dma((BLOCKS,)),
         ],
         compiler_params=pltpu.CompilerParams(
-            collective_id=0, has_side_effects=True, vmem_limit_bytes=48 << 20
+            collective_id=0, has_side_effects=True, vmem_limit_bytes=24 << 20
         ),
         name="exchange",
     )(
-        charges,
-        jnp.transpose(points, (1, 0, 2)),
-        near_target.T,
-        far_target.T,
-        cluster_transfer,
-        bases,
-        leaf_transfer,
+        *in_hbm(
+            charges,
+            jnp.transpose(points, (1, 0, 2)),
+            near_target.T,
+            far_target.T,
+            cluster_transfer,
+            jnp.swapaxes(leaf_bases, 1, 2),
+            leaf_transfer,
+        )
     )
     return pl.pallas_call(
         local_kernel,
         out_shape=jax.ShapeDtypeStruct((LEAVES, POINTS), F32),
-        in_specs=[smem] * 5 + [vmem] * 8 + [anywhere] * 5,
+        in_specs=[vmem] * 9 + [anywhere] * 9,
         out_specs=vmem,
         scratch_shapes=[
             pltpu.VMEM((LEAVES, POINTS, 128), F32),
-            pltpu.VMEM((LEAVES, FAR, RANK, RANK), F32),
-            pltpu.VMEM((LEAVES, RANK, POINTS), F32),
-            pltpu.VMEM((LEAVES, RANK, RANK), F32),
+            pltpu.VMEM((POINTS, POINTS), F32),
+            pltpu.VMEM((LEAVES * FAR + 1, RANK, RANK), F32),
+            pltpu.VMEM((1, RANK, RANK), F32),
+            pltpu.VMEM((1, 8, RANK, RANK), F32),
+            pltpu.VMEM((1, 8, RANK, RANK), F32),
             pltpu.VMEM((32, RANK, RANK), F32),
             pltpu.VMEM((4, RANK, RANK), F32),
             pltpu.VMEM((32, RANK), F32),
             pltpu.VMEM((8, RANK), F32),
+            pltpu.SMEM((2, PAIRS + 128), jnp.int32),
+            pltpu.SMEM((FAR, LEAVES), jnp.int32),
+            pltpu.SMEM((1, 8), jnp.int32),
+            pltpu.SMEM((1, 8), jnp.int32),
+            pltpu.SMEM((4, 8), jnp.int32),
             dma((LEAVES,)),
-            dma((4,)),
+            dma((10,)),
         ],
-        compiler_params=pltpu.CompilerParams(vmem_limit_bytes=62 << 20),
+        compiler_params=pltpu.CompilerParams(vmem_limit_bytes=49 << 20),
         name="local",
     )(
-        pairs, far, cluster_target, group_target, top_target,
-        source, target, all_charges, moments, every,
-        cluster_transfer, cluster_coupling, group_coupling,
-        bases, leaf_transfer, group_transfer, top_coupling, leaf_coupling,
+        *[pltpu.with_memory_space_constraint(array, pltpu.VMEM) for array in handed],
+        *in_hbm(
+            cluster_target,
+            group_target,
+            top_target.T,
+            cluster_transfer,
+            cluster_coupling,
+            group_coupling,
+            group_transfer,
+            top_coupling,
+            leaf_coupling.reshape(LEAVES * FAR, RANK, RANK),
+        ),
     )
 
 

time: 77.5 us -> 50.3 us (0.65)
  Pallas kernels: 64.9 us -> 49.6 us
  local copies, waits for them, and re-layouts: 11.6 us -> 0 us
    pallas_call x1, Pallas kernels: 39.3 us -> 26.1 us  [local(): pl.pallas_call(local_kernel, out_shape=jax.ShapeDtypeStruct((LEAVES, POIN...]
    unnamed x25 -> x0, local copies, waits for them, and re-layouts: 11.6 us -> none
    pallas_call x1, Pallas kernels: 25.6 us -> 23.5 us  [local(): pl.pallas_call(exchange_kernel, out_shape=(pltpu.VMEM((3 * LEAVES + 1, TE...]
where the time goes in v1:
time: 50.3 us; the launch traced here: 49.6 us
  Pallas kernels  49.6 us (99%)
    pallas_call x1, Pallas kernels, local(): pl.pallas_call(local_kernel, out_shape=jax.ShapeDtypeStruct((LEAVES, POIN...  26.1 us
    pallas_call x1, Pallas kernels, local(): pl.pallas_call(exchange_kernel, out_shape=(pltpu.VMEM((3 * LEAVES + 1, TE...  23.5 us

profile of v1, /device:TPU:1, one launch (start us, length us, event | category | flops | bytes accessed | tf_op | source)
XLA Modules:
  0.0 49.6 jit_solution(14231570253089341385)
XLA Ops:
  0.0 23.5 %exchange.1 = (bf16[193,32,256]{2,1,0:T(8,128)(2,1)S(1)}, bf16[64,256,32]{2,1,0:T(8,128)(2,1)S(1)}, f32[200,256]{1,0:T(8,128)S(1)}, f32[328,64]{1,0:T(8,128)S(1)...) custom-call(f32[64,256]{1,0:T(8,128)} %charges_hbm.1, ...), custom_call_target="tpu_custom_call" | custom-call | tf_op jit(solution)/shard_map/exchange/pallas_call | solution.py:476
  23.5 26.1 %local.1 = f32[64,256]{1,0:T(8,128)} custom-call(bf16[193,32,256]{2,1,0:T(8,128)(2,1)S(1)} %get-tuple-element.14.source, bf16[64,256,32]{2,1,0:T(8,128)(2,1)S(1)} %get-tuple-element.15.target, f32[200,256]{1,0:T(8,128)S(1)} %get-tuple-element.16.charges, f32[328,64]{1,0:T(8,128)S(1)} %get-tuple-element.17.moments, ...), custom_call_target="tpu_custom_call" | custom-call | tf_op jit(solution)/shard_map/local/pallas_call | solution.py:527

commit v2 on v1

--- a/solution.py
+++ b/solution.py
@@ -21,9 +21,11 @@
 FAR = 16
 TERMS = 32
 PAIRS = LEAVES * NEAR
-GROUP = 8
+GROUP = 16
+OWN = 2
 CHUNK = 8
-FAR_LEAVES = 2
+RING = 32
+FAR_LEAVES = 8
 DEVICES = 128
 BLOCK = 8
 BLOCKS = DEVICES // BLOCK
@@ -79,11 +81,21 @@
     return jnp.sum(unit * column, axis=0, keepdims=True)
 
 
+def near_group(g, pair):
+    for k in range(GROUP):
+        pair(g * GROUP + k)
+
+
+def folded(square, charge):
+    weighted = lax.rsqrt(square) * charge
+    return weighted[:, :128] + weighted[:, 128:]
+
+
 def exchange_kernel(
     charges_hbm, points_hbm, near_hbm, far_hbm, cluster_transfer_hbm, bases_hbm, transfer_hbm,
-    source_out, target_out, charge_out, moment_out, every_out, far_out, pair_out, bases, transfer,
-    charges, points, near, far, cluster_transfer, halo_charges, halo_points, window, every,
-    load_sems, small_sems, halo_send, halo_recv, moment_send, moment_recv, one_send, one_recv, two_send, two_recv,
+    source_out, target_out, charge_out, moment_out, every_out, far_out, pair_out, bases, transfer, near_out,
+    choice_vector, choice, charges, points, near, far, cluster_transfer, halo_charges, halo_points, window, every,
+    choice_sem, load_sems, small_sems, halo_send, halo_recv, moment_send, moment_recv, one_send, one_recv, two_send, two_recv,
 ):
     gx, gy = lax.axis_index("gx"), lax.axis_index("gy")
     device = gx * 4 + gy
@@ -145,116 +157,27 @@
 
     for copy in small:
         copy.wait()
-    pl.semaphore_wait(barrier, 4 + BLOCK - 1 + BLOCKS - 1)
-
-    def halo_copies():
-        copies = []
-        for side, distance in ((0, 1), (1, -1)):
-            for kind, (source, landing) in enumerate(((charges, halo_charges), (points, halo_points))):
-                copies.append(
-                    pltpu.make_async_remote_copy(
-                        src_ref=source,
-                        dst_ref=landing.at[side],
-                        send_sem=halo_send.at[side, kind],
-                        recv_sem=halo_recv.at[side, kind],
-                        device_id=beside(distance),
-                        device_id_type=MESH,
-                    )
-                )
-        return copies
-
-    halo = halo_copies()
-    for copy in halo:
-        copy.start()
-
-    lane = lax.broadcasted_iota(jnp.int32, (RANK, LEAVES), 1)
-
-    def moment_chunk(c, carry):
-        columns, total = carry
-        for copy in load_copies(c):
-            copy.wait()
-        weights = charges[pl.ds(pl.multiple_of(c * CHUNK, CHUNK), CHUNK), :]
-        for k in range(CHUNK):
-            product = bases[c * CHUNK + k] * weights[k : k + 1, :]
-            column = jnp.sum(product[:, :128] + product[:, 128:], axis=1, keepdims=True)
-            columns = jnp.where(lane == c * CHUNK + k, column, columns)
-            total = total + transfer[c * CHUNK + k] * column
-        return columns, total
-
-    columns, total = lax.fori_loop(
-        0, chunks, moment_chunk, (jnp.zeros((RANK, LEAVES), F32), jnp.zeros((RANK, RANK), F32))
-    )
-    window[2] = columns.T
-    unit = eye()
-    cluster_row = jnp.sum(total, axis=0, keepdims=True)
-    lifted_row = jnp.sum(cluster_transfer[0] * to_column(cluster_row, unit), axis=0, keepdims=True)
-    every[device, 0:1, 0:RANK] = cluster_row
-    every[device, 0:1, RANK : 2 * RANK] = lifted_row
-
-    def one_copy(k):
-        return pltpu.make_async_remote_copy(
-            src_ref=every.at[device],
-            dst_ref=every.at[device],
-            send_sem=one_send.at[k],
-            recv_sem=one_recv.at[k],
-            device_id=block_mate(k),
-            device_id_type=MESH,
-        )
-
-    def two_copy(k):
-        rows = pl.ds(block * BLOCK, BLOCK)
-        return pltpu.make_async_remote_copy(
-            src_ref=every.at[rows],
-            dst_ref=every.at[rows],
-            send_sem=two_send.at[k],
-            recv_sem=two_recv.at[k],
-            device_id=far_mate(k),
-            device_id_type=MESH,
-        )
-
-    @pl.loop(1, BLOCK)
-    def _(k):
-        one_copy(k).start()
-
-    def moment_copies():
-        copies = []
-        for n, distance in enumerate((2, 1, -1, -2)):
-            slot = (0, 1, 3, 4)[n]
-            copies.append(
-                pltpu.make_async_remote_copy(
-                    src_ref=window.at[2],
-                    dst_ref=window.at[slot],
-                    send_sem=moment_send.at[n],
-                    recv_sem=moment_recv.at[n],
-                    device_id=beside(distance),
-                    device_id_type=MESH,
-                )
-            )
-        return copies
-
-    moments = moment_copies()
-    for copy in moments:
-        copy.start()
-
-    @pl.loop(0, chunks)
-    def _(c):
-        span = pl.ds(pl.multiple_of(c * CHUNK, CHUNK), CHUNK)
-        parts, norm = centred([points[n, span, :] for n in range(3)])
-        source_out[pl.ds(LEAVES + c * CHUNK, CHUNK)] = by_leaf(source_terms(parts, norm)).astype(BF16)
-        target = by_leaf(target_terms(parts, norm))
-        for k in range(CHUNK):
-            target_out[c * CHUNK + k] = target[k].T.astype(BF16)
-
-    charge_out[LEAVES : 2 * LEAVES] = charges[...]
-    charge_out[3 * LEAVES :] = jnp.zeros((8, POINTS), F32)
-    term = lax.broadcasted_iota(jnp.int32, (TERMS, POINTS), 0)
-    source_out[BLANK] = jnp.where(term == 18, 1.0, 0.0).astype(BF16)
-
     far_targets = far[...]
     far_out[...] = jnp.where(far_targets >= 0, far_targets - (device - 2) * LEAVES, 5 * LEAVES)
 
     slots = near[...]
-    live = (slots >= 0).astype(F32)
+    local_slots = slots - device * LEAVES
+    own = jnp.where((local_slots >= 0) & (local_slots < LEAVES), 1, 0)
+    live_rows = []
+    own_before = jnp.zeros((1, LEAVES), jnp.int32)
+    chosen = [jnp.full((1, LEAVES), BLANK, jnp.int32) for _ in range(OWN)]
+    for s in range(NEAR):
+        is_own = own[s : s + 1] > 0
+        for n in range(OWN):
+            chosen[n] = jnp.where(is_own & (own_before == n), local_slots[s : s + 1] + LEAVES, chosen[n])
+        left = jnp.where(is_own & (own_before < OWN), 0.0, 1.0)
+        live_rows.append(jnp.where(slots[s : s + 1] >= 0, left, 0.0))
+        own_before = own_before + own[s : s + 1]
+    for n in range(OWN):
+        choice_vector[n : n + 1, 0:LEAVES] = chosen[n]
+    choice_copy = pltpu.make_async_copy(choice_vector, choice, choice_sem)
+    choice_copy.start()
+    live = jnp.concatenate(live_rows, axis=0)
     before = (
         lax.broadcasted_iota(jnp.int32, (LEAVES, LEAVES), 0) < lax.broadcasted_iota(jnp.int32, (LEAVES, LEAVES), 1)
     ).astype(BF16)
@@ -280,13 +203,141 @@
         [far_live, jnp.broadcast_to(start.astype(jnp.int32), (1, PAIRS - LEAVES))], axis=1
     )
 
+    pl.semaphore_wait(barrier, 4 + BLOCK - 1 + BLOCKS - 1)
+
+    def halo_copies():
+        copies = []
+        for side, distance in ((0, 1), (1, -1)):
+            for kind, (source, landing) in enumerate(((charges, halo_charges), (points, halo_points))):
+                copies.append(
+                    pltpu.make_async_remote_copy(
+                        src_ref=source,
+                        dst_ref=landing.at[side],
+                        send_sem=halo_send.at[side, kind],
+                        recv_sem=halo_recv.at[side, kind],
+                        device_id=beside(distance),
+                        device_id_type=MESH,
+                    )
+                )
+        return copies
+
+    halo = halo_copies()
+    for copy in halo:
+        copy.start()
+
+    lane = lax.broadcasted_iota(jnp.int32, (RANK, LEAVES), 1)
+
+    def moment_chunk(c, carry):
+        columns, total = carry
+        for copy in load_copies(c):
+            copy.wait()
+        weights = charges[pl.ds(pl.multiple_of(c * CHUNK, CHUNK), CHUNK), :]
+        for k in range(CHUNK):
+            product = bases[c * CHUNK + k] * weights[k : k + 1, :]
+            column = jnp.sum(product[:, :128] + product[:, 128:], axis=1, keepdims=True)
+            columns = jnp.where(lane == c * CHUNK + k, column, columns)
+            total = total + transfer[c * CHUNK + k] * column
+        return columns, total
+
+    columns, total = lax.fori_loop(
+        0, chunks, moment_chunk, (jnp.zeros((RANK, LEAVES), F32), jnp.zeros((RANK, RANK), F32))
+    )
+    moment_rows = columns.T
+    window[2] = jnp.concatenate([moment_rows[: LEAVES // 2], moment_rows[LEAVES // 2 :]], axis=1)
+    unit = eye()
+    cluster_row = jnp.sum(total, axis=0, keepdims=True)
+    lifted_row = jnp.sum(cluster_transfer[0] * to_column(cluster_row, unit), axis=0, keepdims=True)
+    every[device, 0:1, 0:RANK] = cluster_row
+    every[device, 0:1, RANK : 2 * RANK] = lifted_row
+
+    def one_copy(k):
+        return pltpu.make_async_remote_copy(
+            src_ref=every.at[device],
+            dst_ref=every.at[device],
+            send_sem=one_send.at[k],
+            recv_sem=one_recv.at[k],
+            device_id=block_mate(k),
+            device_id_type=MESH,
+        )
+
+    def two_copy(k):
+        rows = pl.ds(block * BLOCK, BLOCK)
+        return pltpu.make_async_remote_copy(
+            src_ref=every.at[rows],
+            dst_ref=every.at[rows],
+            send_sem=two_send.at[k],
+            recv_sem=two_recv.at[k],
+            device_id=far_mate(k),
+            device_id_type=MESH,
+        )
+
     @pl.loop(1, BLOCK)
     def _(k):
+        one_copy(k).start()
+
+    def moment_copies():
+        copies = []
+        for n, distance in enumerate((2, 1, -1, -2)):
+            slot = (0, 1, 3, 4)[n]
+            copies.append(
+                pltpu.make_async_remote_copy(
+                    src_ref=window.at[2],
+                    dst_ref=window.at[slot],
+                    send_sem=moment_send.at[n],
+                    recv_sem=moment_recv.at[n],
+                    device_id=beside(distance),
+                    device_id_type=MESH,
+                )
+            )
+        return copies
+
+    moments = moment_copies()
+    for copy in moments:
+        copy.start()
+
+    @pl.loop(0, chunks)
+    def _(c):
+        span = pl.ds(pl.multiple_of(c * CHUNK, CHUNK), CHUNK)
+        parts, norm = centred([points[n, span, :] for n in range(3)])
+        source_out[pl.ds(LEAVES + c * CHUNK, CHUNK)] = by_leaf(source_terms(parts, norm)).astype(BF16)
+        target = by_leaf(target_terms(parts, norm))
+        for k in range(CHUNK):
+            target_out[c * CHUNK + k] = target[k].T.astype(BF16)
+
+    charge_out[LEAVES : 2 * LEAVES] = charges[...]
+    charge_out[3 * LEAVES :] = jnp.zeros((8, POINTS), F32)
+    term = lax.broadcasted_iota(jnp.int32, (TERMS, POINTS), 0)
+    source_out[BLANK] = jnp.where(term == 18, 1.0, 0.0).astype(BF16)
+
+    choice_copy.wait()
+
+    def own_pair(n, i):
+        j = jnp.clip(choice[n, i], 0, BLANK)
+        part = folded(
+            jnp.dot(target_out[i], source_out[j], preferred_element_type=F32), charge_out[pl.ds(j, 1), :]
+        )
+        if n == 0:
+            near_out[i] = part
+        else:
+            near_out[i] += part
+
+    @pl.loop(0, LEAVES // GROUP)
+    def _(g):
+        near_group(g, functools.partial(own_pair, 0))
+
+    @pl.loop(1, BLOCK)
+    def _(k):
         one_copy(k).wait_recv()
 
     @pl.loop(1, BLOCKS)
     def _(k):
         two_copy(k).start()
+
+    for n in range(1, OWN):
+
+        @pl.loop(0, LEAVES // GROUP)
+        def _(g):
+            near_group(g, functools.partial(own_pair, n))
 
     for side in range(2):
         halo[2 * side].wait_recv()
@@ -304,7 +355,8 @@
     for copy in moments:
         copy.wait_recv()
     for n in range(5):
-        moment_out[n * LEAVES : (n + 1) * LEAVES] = window[n]
+        moment_out[n * LEAVES : n * LEAVES + LEAVES // 2] = window[n][:, :RANK]
+        moment_out[n * LEAVES + LEAVES // 2 : (n + 1) * LEAVES] = window[n][:, RANK:]
     moment_out[5 * LEAVES :] = jnp.zeros((8, RANK), F32)
 
     @pl.loop(1, BLOCKS)
@@ -326,11 +378,11 @@
 
 
 def local_kernel(
-    source, target, charges, moments, every, far_vmem, pairs_vmem, bases, transfer,
+    source, target, charges, moments, every, far_vmem, pairs_vmem, bases, transfer, near_first,
     cluster_target_hbm, group_target_hbm, top_target_hbm, cluster_transfer_hbm, cluster_coupling_hbm,
     group_coupling_hbm, group_transfer_hbm, top_coupling_hbm, coupling_hbm,
     out,
-    near_total, ahead, coupling, cluster_transfer, cluster_coupling, group_coupling, group_transfer, top_coupling,
+    near_total, parts, coupling, far_total, cluster_transfer, cluster_coupling, group_coupling, group_transfer, top_coupling,
     group_moments, top_moments, pairs, far, cluster_target, group_target, top_target,
     coupling_sems, sems,
 ):
@@ -360,60 +412,78 @@
     @pl.loop(0, LEAVES // 4)
     def _(c):
         for k in range(4):
-            near_total[c * 4 + k] = jnp.zeros((POINTS, 128), F32)
-
-    coupling[LEAVES * FAR] = jnp.zeros((RANK, RANK), F32)
+            near_total[c * 4 + k] = near_first[c * 4 + k]
+
+    for k in range(GROUP):
+        parts[k] = jnp.zeros((POINTS, 128), F32)
+
+    coupling[RING * FAR] = jnp.zeros((RANK, RANK), F32)
     for copy in loads[:2]:
         copy.wait()
 
     def coupling_copy(i):
         count = jnp.maximum(pairs[1, i], 1)
         return pltpu.make_async_copy(
-            coupling_hbm.at[pl.ds(i * FAR, count)], coupling.at[pl.ds(i * FAR, count)], coupling_sems.at[i]
-        )
-
-    @pl.loop(0, LEAVES)
+            coupling_hbm.at[pl.ds(i * FAR, count)],
+            coupling.at[pl.ds((i % RING) * FAR, count)],
+            coupling_sems.at[i % RING],
+        )
+
+    @pl.loop(0, RING)
     def _(i):
         coupling_copy(i).start()
 
-    def squares(p):
-        code = pairs[0, p]
-        return jnp.dot(target[code // 256], source[code % 256], preferred_element_type=F32)
-
-    def add_near(p, square):
-        code = pairs[0, p]
-        weighted = lax.rsqrt(square) * charges[pl.ds(code % 256, 1), :]
-        near_total[code // 256] += weighted[:, :128] + weighted[:, 128:]
-
-    def near_group(g):
-        add_near(g * GROUP, ahead[...])
-        for k in range(1, GROUP):
-            add_near(g * GROUP + k, squares(g * GROUP + k))
-        ahead[...] = squares(g * GROUP + GROUP)
+    def add_parts(g):
+        for k in range(GROUP):
+            near_total[pairs[0, g * GROUP + k] // 256] += parts[k]
+
+    def listed_group(g, beside):
+        add_parts(jnp.maximum(g - 1, 0))
+        for k in range(GROUP):
+            code = pairs[0, g * GROUP + k]
+            i, j = code // 256, code % 256
+            square = jnp.dot(target[i], source[j], preferred_element_type=F32)
+            parts[k] = folded(square, charges[pl.ds(j, 1), :])
+            beside(k)
 
     def far_leaf(i):
         count = pairs[1, i]
         total = None
         for f in range(FAR):
-            index = jnp.where(f < count, i * FAR + f, LEAVES * FAR)
+            index = jnp.where(f < count, (i % RING) * FAR + f, RING * FAR)
             term = coupling[index] * moments[pl.ds(far[f, i], 1), :]
             total = term if total is None else total + term
-        coupling[i * FAR] = total
-
-    ahead[...] = squares(0)
+        far_total[i] = total
+
     shared = LEAVES // FAR_LEAVES
 
-    @pl.loop(0, shared)
-    def _(g):
+    def far_step(g):
         for k in range(FAR_LEAVES):
             coupling_copy(g * FAR_LEAVES + k).wait()
+
+        def beside(k):
+            if k % (GROUP // FAR_LEAVES) == 0:
+                far_leaf(g * FAR_LEAVES + k // (GROUP // FAR_LEAVES))
+
+        listed_group(g, beside)
+
+    refilled = shared - RING // FAR_LEAVES
+
+    @pl.loop(0, refilled)
+    def _(g):
+        far_step(g)
         for k in range(FAR_LEAVES):
-            far_leaf(g * FAR_LEAVES + k)
-        near_group(g)
-
-    @pl.loop(shared, jnp.maximum((pairs[1, LEAVES] + GROUP - 1) // GROUP, shared))
+            coupling_copy(g * FAR_LEAVES + k + RING).start()
+
+    @pl.loop(refilled, shared)
     def _(g):
-        near_group(g)
+        far_step(g)
+
+    groups = jnp.maximum((pairs[1, LEAVES] + GROUP - 1) // GROUP, shared + 1)
+
+    @pl.loop(shared, groups - 1)
+    def _(g):
+        listed_group(g, lambda k: None)
 
     unit = eye()
     for copy in loads[2:]:
@@ -449,17 +519,30 @@
         total = total + cluster_coupling[0, f] * (every[t, :, :RANK] * weight)
     cluster_local = to_row(jnp.sum(total, axis=1, keepdims=True), unit)
 
+    listed_group(groups - 1, lambda k: None)
+    add_parts(groups - 1)
+
+    lane = lax.broadcasted_iota(jnp.int32, (POINTS, 128), 1)
+
+    def merged(first, second, distance):
+        here = (lane & distance) == 0
+        return jnp.where(here, first, second) + pltpu.roll(jnp.where(here, second, first), 128 - distance, axis=1)
+
     @pl.loop(0, LEAVES // CHUNK)
     def _(c):
         rows = []
         for k in range(CHUNK):
             i = c * CHUNK + k
-            total = transfer[i] * cluster_local + coupling[i * FAR]
+            total = transfer[i] * cluster_local + far_total[i]
             leaf_local = jnp.sum(total, axis=1, keepdims=True)
-            far_part = jnp.sum(bases[i] * leaf_local, axis=0, keepdims=True)
-            near_part = jnp.sum(near_total[i].T, axis=0, keepdims=True)
-            rows.append(near_part * INVERSE_FOUR_PI + far_part)
-        out[pl.ds(pl.multiple_of(c * CHUNK, CHUNK), CHUNK), :] = jnp.concatenate(rows, axis=0)
+            rows.append(jnp.sum(bases[i] * leaf_local, axis=0, keepdims=True))
+        totals = [near_total[c * CHUNK + k] for k in range(CHUNK)]
+        for distance in (1, 2, 4):
+            totals = [merged(totals[n], totals[n + 1], distance) for n in range(0, len(totals), 2)]
+        near_part = jnp.sum(totals[0].T.reshape(128 // CHUNK, CHUNK, POINTS), axis=0)
+        out[pl.ds(pl.multiple_of(c * CHUNK, CHUNK), CHUNK), :] = near_part * INVERSE_FOUR_PI + jnp.concatenate(
+            rows, axis=0
+        )
 
 
 def local(
@@ -485,10 +568,13 @@
             pltpu.VMEM((2, PAIRS + 128), jnp.int32),
             pltpu.VMEM((LEAVES, RANK, POINTS), F32),
             pltpu.VMEM((LEAVES, RANK, RANK), F32),
+            pltpu.VMEM((LEAVES, POINTS, 128), F32),
         ),
         in_specs=[anywhere] * 7,
-        out_specs=[vmem] * 9,
+        out_specs=[vmem] * 10,
         scratch_shapes=[
+            pltpu.VMEM((8, 128), jnp.int32),
+            pltpu.SMEM((8, 128), jnp.int32),
             pltpu.VMEM((LEAVES, POINTS), F32),
             pltpu.VMEM((3, LEAVES, POINTS), F32),
             pltpu.VMEM((NEAR, LEAVES), jnp.int32),
@@ -496,8 +582,9 @@
             pltpu.VMEM((1, RANK, RANK), F32),
             pltpu.VMEM((2, LEAVES, POINTS), F32),
             pltpu.VMEM((2, 3, LEAVES, POINTS), F32),
-            pltpu.VMEM((5, LEAVES, RANK), F32),
+            pltpu.VMEM((5, LEAVES // 2, 2 * RANK), F32),
             pltpu.VMEM((DEVICES, 1, 2 * RANK), F32),
+            dma,
             dma((2, LEAVES // CHUNK)),
             dma((5,)),
             dma((2, 2)),
@@ -510,7 +597,7 @@
             dma((BLOCKS,)),
         ],
         compiler_params=pltpu.CompilerParams(
-            collective_id=0, has_side_effects=True, vmem_limit_bytes=24 << 20
+            collective_id=0, has_side_effects=True, vmem_limit_bytes=32 << 20
         ),
         name="exchange",
     )(
@@ -527,12 +614,13 @@
     return pl.pallas_call(
         local_kernel,
         out_shape=jax.ShapeDtypeStruct((LEAVES, POINTS), F32),
-        in_specs=[vmem] * 9 + [anywhere] * 9,
+        in_specs=[vmem] * 10 + [anywhere] * 9,
         out_specs=vmem,
         scratch_shapes=[
             pltpu.VMEM((LEAVES, POINTS, 128), F32),
-            pltpu.VMEM((POINTS, POINTS), F32),
-            pltpu.VMEM((LEAVES * FAR + 1, RANK, RANK), F32),
+            pltpu.VMEM((GROUP, POINTS, 128), F32),
+            pltpu.VMEM((RING * FAR + 1, RANK, RANK), F32),
+            pltpu.VMEM((LEAVES, RANK, RANK), F32),
             pltpu.VMEM((1, RANK, RANK), F32),
             pltpu.VMEM((1, 8, RANK, RANK), F32),
             pltpu.VMEM((1, 8, RANK, RANK), F32),
@@ -545,10 +633,10 @@
             pltpu.SMEM((1, 8), jnp.int32),
             pltpu.SMEM((1, 8), jnp.int32),
             pltpu.SMEM((4, 8), jnp.int32),
-            dma((LEAVES,)),
+            dma((RING,)),
             dma((10,)),
         ],
-        compiler_params=pltpu.CompilerParams(vmem_limit_bytes=49 << 20),
+        compiler_params=pltpu.CompilerParams(vmem_limit_bytes=36 << 20),
         name="local",
     )(
         *[pltpu.with_memory_space_constraint(array, pltpu.VMEM) for array in handed],

time: 50.3 us -> 52.6 us (1.046); the launches traced: 49.6 us -> 52.5 us
  local copies, waits for them, and re-layouts: 0 us -> 7.7 us
  Pallas kernels: 49.6 us -> 44.8 us
    unnamed x0 -> x8, local copies, waits for them, and re-layouts: none -> 7.7 us
    pallas_call x1, Pallas kernels: 26.1 us -> 20.6 us  [local(): pl.pallas_call(local_kernel, out_shape=jax.ShapeDtypeStruct((LEAVES, POIN...]
    pallas_call x1, Pallas kernels: 23.5 us -> 24.2 us  [local(): pl.pallas_call(exchange_kernel, out_shape=(pltpu.VMEM((3 * LEAVES + 1, TE...]
where the time goes in v2:
time: 52.6 us; the launch traced here: 52.5 us
  Pallas kernels  44.8 us (85%)
  local copies, waits for them, and re-layouts  7.7 us (15%)
    pallas_call x1, Pallas kernels, local(): pl.pallas_call(exchange_kernel, out_shape=(pltpu.VMEM((3 * LEAVES + 1, TE...  24.2 us
    pallas_call x1, Pallas kernels, local(): pl.pallas_call(local_kernel, out_shape=jax.ShapeDtypeStruct((LEAVES, POIN...  20.6 us
    unnamed x8, local copies, waits for them, and re-layouts  7.7 us

profile of v2, /device:TPU:1, one launch (start us, length us, event | category | flops | bytes accessed | tf_op | source)
XLA Modules:
  0.0 52.5 jit_solution(2085930032816933107)
XLA Ops:
  0.0 24.2 %exchange.1 = (bf16[193,32,256]{2,1,0:T(8,128)(2,1)S(1)}, bf16[64,256,32]{2,1,0:T(8,128)(2,1)S(1)}, f32[200,256]{1,0:T(8,128)S(1)}, f32[328,64]{1,0:T(8,128)S(1)...) custom-call(f32[64,256]{1,0:T(8,128)} %charges_hbm.1, ...), custom_call_target="tpu_custom_call" | custom-call | tf_op jit(solution)/shard_map/exchange/pallas_call | solution.py:559
  24.2 0.0 copy-start
  24.2 1.9 %copy-done = f32[64,64,256]{2,1,0:T(8,128)} copy-done((f32[64,64,256]{2,1,0:T(8,128)}, f32[64,64,256]{2,1,0:T(8,128)S(1)}, u32[]{:S(2)}) %copy-start) | copy-done | bytes 4194328
  26.1 0.0 copy-start.2
  26.1 1.7 %copy-done.2 = bf16[193,32,256]{2,1,0:T(8,128)(2,1)} copy-done((bf16[193,32,256]{2,1,0:T(8,128)(2,1)}, bf16[193,32,256]{2,1,0:T(8,128)(2,1)S(1)}, u32[]{:S(2)}) %copy-start.2) | copy-done | bytes 3162136
  27.8 0.0 copy-start.1
  27.8 2.2 %copy-done.1 = f32[64,64,256]{2,1,0:T(8,128)S(1)} copy-done((f32[64,64,256]{2,1,0:T(8,128)S(1)}, f32[64,64,256]{2,1,0:T(8,128)}, u32[]{:S(2)}) %copy-start.1) | copy-done | bytes 4194328
  30.0 0.0 copy-start.3
  30.0 1.9 %copy-done.3 = bf16[193,32,256]{2,1,0:T(8,128)(2,1)S(1)} copy-done((bf16[193,32,256]{2,1,0:T(8,128)(2,1)S(1)}, bf16[193,32,256]{2,1,0:T(8,128)(2,1)}, u32[]{:S(2)}) %copy-start.3) | copy-done | bytes 3162136
  31.9 20.6 %local.1 = f32[64,256]{1,0:T(8,128)} custom-call(bf16[193,32,256]{2,1,0:T(8,128)(2,1)S(1)} %copy-done.3, bf16[64,256,32]{2,1,0:T(8,128)(2,1)S(1)} %get-tuple-element.16.target, f32[200,256]{1,0:T(8,128)S(1)} %get-tuple-element.17.charges, f32[328,64]{1,0:T(8,128)S(1)} %get-tuple-element.18.moments, f32[128,1,128]{2,1,0:T(1,128)S(1)} %get-tuple-element.19.every, ...), custom_call_target="tpu_custom_call" | custom-call | tf_op jit(solution)/shard_map/local/pallas_call | solution.py:614
Async XLA Ops:
  24.2 1.9 %copy-start = (f32[64,64,256]{2,1,0:T(8,128)}, f32[64,64,256]{2,1,0:T(8,128)S(1)}, u32[]{:S(2)}) copy-start(f32[64,64,256]{2,1,0:T(8,128)S(1)} %get-tuple-element.22.bases) | copy-start | bytes 12582916
  26.1 1.7 %copy-start.2 = (bf16[193,32,256]{2,1,0:T(8,128)(2,1)}, bf16[193,32,256]{2,1,0:T(8,128)(2,1)S(1)}, u32[]{:S(2)}) copy-start(bf16[193,32,256]{2,1,0:T(8,128)(2,1)S(1)} %get-tuple-element.15.source) | copy-start | bytes 9486340
  27.8 2.2 %copy-start.1 = (f32[64,64,256]{2,1,0:T(8,128)S(1)}, f32[64,64,256]{2,1,0:T(8,128)}, u32[]{:S(2)}) copy-start(f32[64,64,256]{2,1,0:T(8,128)} %copy-done) | copy-start | bytes 12582916
  30.0 1.9 %copy-start.3 = (bf16[193,32,256]{2,1,0:T(8,128)(2,1)S(1)}, bf16[193,32,256]{2,1,0:T(8,128)(2,1)}, u32[]{:S(2)}) copy-start(bf16[193,32,256]{2,1,0:T(8,128)(2,1)} %copy-done.2) | copy-start | bytes 9486340

commit v3 on v2

v3 whole, which is shorter than its diff:
```python
import functools
import math

import jax
import jax.numpy as jnp
from jax import lax
from jax.experimental import pallas as pl
from jax.experimental.pallas import tpu as pltpu
from jax.sharding import PartitionSpec as P

MESH = pl.DeviceIdType.MESH
F32 = jnp.float32
BF16 = jnp.bfloat16
SMOOTHING = 0.01
INVERSE_FOUR_PI = 1.0 / (4.0 * math.pi)

LEAVES = 64
POINTS = 256
RANK = 64
NEAR = 8
FAR = 16
TERMS = 32
PAIRS = LEAVES * NEAR
GROUP = 16
OWN = 1
CHUNK = 8
DEVICES = 128
STAGES = ((1, 4), (4, 4), (16, 8))
HALO_PARTS = 2
BLANK = 3 * LEAVES


def split3(value):
    high = value.astype(BF16).astype(F32)
    rest = value - high
    middle = rest.astype(BF16).astype(F32)
    low = (rest - middle).astype(BF16).astype(F32)
    return high, middle, low


def centred(points):
    shifted = [p - 1.0 for p in points]
    norm = shifted[0] * shifted[0] + shifted[1] * shifted[1] + shifted[2] * shifted[2]
    return [split3(u) for u in shifted], norm


def source_terms(parts, norm):
    rows = []
    for high, middle, low in parts:
        high, middle, low = -2.0 * high, -2.0 * middle, -2.0 * low
        rows += [high, high, high, middle, middle, low]
    one = jnp.ones_like(norm)
    return rows + list(split3(norm + SMOOTHING)) + [one, one, one]


def target_terms(parts, norm):
    rows = []
    for high, middle, low in parts:
        rows += [high, middle, low, high, middle, high]
    one = jnp.ones_like(norm)
    return rows + [one, one, one] + list(split3(norm))


def by_leaf(rows):
    blank = jnp.zeros_like(rows[0])
    return jnp.swapaxes(jnp.stack(rows + [blank] * (TERMS - len(rows)), axis=0), 0, 1)


def eye():
    shape = (RANK, RANK)
    return (lax.broadcasted_iota(jnp.int32, shape, 0) == lax.broadcasted_iota(jnp.int32, shape, 1)).astype(F32)


def to_column(row, unit):
    return jnp.sum(unit * row, axis=1, keepdims=True)


def to_row(column, unit):
    return jnp.sum(unit * column, axis=0, keepdims=True)


def merged(first, second, distance):
    lane = lax.broadcasted_iota(jnp.int32, first.shape, 1)
    here = (lane & distance) == 0
    return jnp.where(here, first, second) + pltpu.roll(jnp.where(here, second, first), 128 - distance, axis=1)


def lane_sums(parts):
    parts = [parts[k] for k in range(CHUNK)]
    for distance in (1, 2, 4):
        parts = [merged(parts[n], parts[n + 1], distance) for n in range(0, len(parts), 2)]
    return jnp.sum(parts[0].T.reshape(128 // CHUNK, CHUNK, POINTS), axis=0)


def folded(square, charge):
    weighted = lax.rsqrt(square) * charge
    return weighted[:, :128] + weighted[:, 128:]


def exchange_kernel(
    charges_hbm, points_hbm, near_hbm, far_hbm, cluster_transfer_hbm, bases_hbm, transfer_hbm, coupling_hbm,
    source_out, target_out, charge_out, every_out, pair_out, bases, transfer, near_out, far_out,
    coupling, far_vector, far_rows, moment_rows, choice_vector, choice, own, near, far, cluster_transfer, halo, window, every,
    coupling_sems, far_sem, choice_sem, load_sems, small_sems, halo_send, halo_recv, moment_send, moment_recv, every_send, every_recv,
):
    gx, gy = lax.axis_index("gx"), lax.axis_index("gy")
    device = gx * 4 + gy

    def place(index):
        return (index // 4, index % 4)

    def beside(distance):
        return place((device + distance + DEVICES) % DEVICES)

    chunks = LEAVES // CHUNK

    def load_copies(c):
        span = pl.ds(c * CHUNK, CHUNK)
        return (
            pltpu.make_async_copy(bases_hbm.at[span], bases.at[span], load_sems.at[0, c]),
            pltpu.make_async_copy(transfer_hbm.at[span], transfer.at[span], load_sems.at[1, c]),
        )

    small = [
        pltpu.make_async_copy(source, landing, small_sems.at[n])
        for n, (source, landing) in enumerate(
            (
                (charges_hbm, own.at[0]),
                (points_hbm, own.at[pl.ds(1, 3)]),
                (near_hbm, near),
                (far_hbm, far),
                (cluster_transfer_hbm, cluster_transfer),
            )
        )
    ]
    for copy in small:
        copy.start()

    @pl.loop(0, chunks)
    def _(c):
        for copy in load_copies(c):
            copy.start()

    def coupling_copy(c):
        span = pl.ds(c * CHUNK * FAR, CHUNK * FAR)
        return pltpu.make_async_copy(coupling_hbm.at[span], coupling.at[span], coupling_sems.at[c])

    @pl.loop(0, chunks)
    def _(c):
        coupling_copy(c).start()

    barrier = pltpu.get_barrier_semaphore()
    for distance in (1, -1, 2, -2):
        pl.semaphore_signal(barrier, inc=1, device_id=beside(distance), device_id_type=MESH)

    def mate(stage, k):
        unit, count = STAGES[stage]
        position = (device // unit) % count
        return place(device + ((position + k) % count - position) * unit)

    for stage in range(len(STAGES)):

        @pl.loop(1, STAGES[stage][1])
        def _(k):
            pl.semaphore_signal(barrier, inc=1, device_id=mate(stage, k), device_id_type=MESH)

    for copy in small:
        copy.wait()
    far_targets = far[...]
    far_vector[...] = jnp.where(far_targets >= 0, far_targets - (device - 2) * LEAVES, 5 * LEAVES).T
    far_copy = pltpu.make_async_copy(far_vector, far_rows, far_sem)
    far_copy.start()

    slots = near[...]
    local_slots = slots - device * LEAVES
    is_here = jnp.where((local_slots >= 0) & (local_slots < LEAVES), 1, 0)
    live_rows = []
    own_before = jnp.zeros((1, LEAVES), jnp.int32)
    chosen = [jnp.full((1, LEAVES), BLANK, jnp.int32) for _ in range(OWN)]
    for s in range(NEAR):
        is_own = is_here[s : s + 1] > 0
        for n in range(OWN):
            chosen[n] = jnp.where(is_own & (own_before == n), local_slots[s : s + 1] + LEAVES, chosen[n])
        left = jnp.where(is_own & (own_before < OWN), 0.0, 1.0)
        live_rows.append(jnp.where(slots[s : s + 1] >= 0, left, 0.0))
        own_before = own_before + is_here[s : s + 1]
    for n in range(OWN):
        choice_vector[n : n + 1, 0:LEAVES] = chosen[n]
    choice_copy = pltpu.make_async_copy(choice_vector, choice, choice_sem)
    choice_copy.start()
    live = jnp.concatenate(live_rows, axis=0)
    before = (
        lax.broadcasted_iota(jnp.int32, (LEAVES, LEAVES), 0) < lax.broadcasted_iota(jnp.int32, (LEAVES, LEAVES), 1)
    ).astype(BF16)
    rank_in_slot = jnp.dot(live.astype(BF16), before, preferred_element_type=F32)
    in_slot = jnp.sum(live, axis=1, keepdims=True)
    leaf_row = lax.broadcasted_iota(jnp.int32, (1, LEAVES), 1)
    code = (leaf_row * 256 + slots - (device - 1) * LEAVES).astype(F32)
    position_row = lax.broadcasted_iota(jnp.int32, (1, PAIRS), 1).astype(F32)
    found = jnp.zeros((LEAVES, PAIRS), F32)
    start = jnp.zeros((1, 1), F32)
    positions = []
    for s in range(NEAR):
        positions.append(jnp.where(live[s : s + 1] > 0, rank_in_slot[s : s + 1] + start, -1.0))
        start = start + in_slot[s : s + 1]
    table = jnp.concatenate(positions + [code], axis=0).T
    for s in range(NEAR):
        found = jnp.where(table[:, s : s + 1] == position_row, table[:, NEAR + s : NEAR + s + 1], found)
    pairs = jnp.sum(found, axis=0, keepdims=True)
    pair_out[0:1, 0:PAIRS] = jnp.where(position_row < start, pairs, float(BLANK)).astype(jnp.int32)
    pair_out[0:1, PAIRS:] = jnp.full((1, 128), BLANK, jnp.int32)
    pair_out[1:2, 0:128] = jnp.broadcast_to(start.astype(jnp.int32), (1, 128))
    pl.semaphore_wait(barrier, 4 + sum(count - 1 for _, count in STAGES))

    part_leaves = LEAVES // HALO_PARTS
    copies_of_halo = [
        [
            pltpu.make_async_remote_copy(
                src_ref=own.at[:, pl.ds(part * part_leaves, part_leaves)],
                dst_ref=halo.at[side, :, pl.ds(part * part_leaves, part_leaves)],
                send_sem=halo_send.at[part, side],
                recv_sem=halo_recv.at[part, side],
                device_id=beside(distance),
                device_id_type=MESH,
            )
            for side, distance in ((0, 1), (1, -1))
        ]
        for part in range(HALO_PARTS)
    ]
    for copies in copies_of_halo:
        for copy in copies:
            copy.start()

    lane = lax.broadcasted_iota(jnp.int32, (RANK, LEAVES), 1)

    def moment_chunk(c, carry):
        columns, total = carry
        for copy in load_copies(c):
            copy.wait()
        weights = own[0, pl.ds(pl.multiple_of(c * CHUNK, CHUNK), CHUNK), :]
        for k in range(CHUNK):
            product = bases[c * CHUNK + k] * weights[k : k + 1, :]
            column = jnp.sum(product[:, :128] + product[:, 128:], axis=1, keepdims=True)
            columns = jnp.where(lane == c * CHUNK + k, column, columns)
            total = total + transfer[c * CHUNK + k] * column
        return columns, total

    columns, total = lax.fori_loop(
        0, chunks, moment_chunk, (jnp.zeros((RANK, LEAVES), F32), jnp.zeros((RANK, RANK), F32))
    )
    rows = columns.T
    window[2] = jnp.concatenate([rows[: LEAVES // 2], rows[LEAVES // 2 :]], axis=1)
    unit = eye()
    cluster_row = jnp.sum(total, axis=0, keepdims=True)
    lifted_row = jnp.sum(cluster_transfer[0] * to_column(cluster_row, unit), axis=0, keepdims=True)
    every[device, 0:1, 0:RANK] = cluster_row
    every[device, 0:1, RANK : 2 * RANK] = lifted_row

    def every_copy(stage, k):
        unit, _ = STAGES[stage]
        rows = pl.ds((device // unit) * unit, unit)
        return pltpu.make_async_remote_copy(
            src_ref=every.at[rows],
            dst_ref=every.at[rows],
            send_sem=every_send.at[stage, k],
            recv_sem=every_recv.at[stage, k],
            device_id=mate(stage, k),
            device_id_type=MESH,
        )

    def start_stage(stage):
        for k in range(1, STAGES[stage][1]):
            every_copy(stage, k).start()

    def finish_stage(stage):
        for k in range(1, STAGES[stage][1]):
            every_copy(stage, k).wait_recv()

    start_stage(0)

    def moment_copies():
        copies = []
        for n, distance in enumerate((2, 1, -1, -2)):
            slot = (0, 1, 3, 4)[n]
            copies.append(
                pltpu.make_async_remote_copy(
                    src_ref=window.at[2],
                    dst_ref=window.at[slot],
                    send_sem=moment_send.at[n],
                    recv_sem=moment_recv.at[n],
                    device_id=beside(distance),
                    device_id_type=MESH,
                )
            )
        return copies

    moments = moment_copies()
    for copy in moments:
        copy.start()

    @pl.loop(0, chunks)
    def _(c):
        span = pl.ds(pl.multiple_of(c * CHUNK, CHUNK), CHUNK)
        parts, norm = centred([own[n, span, :] for n in range(1, 4)])
        source_out[pl.ds(LEAVES + c * CHUNK, CHUNK)] = by_leaf(source_terms(parts, norm)).astype(BF16)
        target = by_leaf(target_terms(parts, norm))
        for k in range(CHUNK):
            target_out[c * CHUNK + k] = target[k].T.astype(BF16)

    charge_out[LEAVES : 2 * LEAVES] = own[0]
    charge_out[3 * LEAVES :] = jnp.zeros((8, POINTS), F32)
    term = lax.broadcasted_iota(jnp.int32, (TERMS, POINTS), 0)
    source_out[BLANK] = jnp.where(term == 18, 1.0, 0.0).astype(BF16)

    finish_stage(0)
    start_stage(1)

    choice_copy.wait()

    @pl.loop(0, LEAVES // GROUP)
    def _(g):
        for k in range(GROUP):
            i = g * GROUP + k
            for n in range(OWN):
                j = jnp.clip(choice[n, i], 0, BLANK)
                square = jnp.dot(target_out[i], source_out[j], preferred_element_type=F32)
                part = folded(square, charge_out[pl.ds(j, 1), :])
                if n == 0:
                    near_out[i] = part
                else:
                    near_out[i] += part

    finish_stage(1)
    start_stage(2)

    for copy in moments:
        copy.wait_recv()
    for n in range(5):
        moment_rows[n * LEAVES : n * LEAVES + LEAVES // 2] = window[n][:, :RANK]
        moment_rows[n * LEAVES + LEAVES // 2 : (n + 1) * LEAVES] = window[n][:, RANK:]
    moment_rows[5 * LEAVES :] = jnp.zeros((8, RANK), F32)
    far_copy.wait()

    def far_chunk(c):
        coupling_copy(c).wait()
        for k in range(CHUNK):
            i = c * CHUNK + k
            total = None
            for f in range(FAR):
                row = jnp.clip(far_rows[i, f], 0, 5 * LEAVES)
                term = coupling[i * FAR + f] * moment_rows[pl.ds(row, 1), :]
                total = term if total is None else total + term
            far_out[i] = total

    early = chunks * 5 // 8
    pl.loop(0, early)(far_chunk)

    for part in range(HALO_PARTS):
        for side in range(2):
            copies_of_halo[part][side].wait_recv()
            first = 2 * LEAVES * side

            @pl.loop(part * part_leaves // CHUNK, (part + 1) * part_leaves // CHUNK)
            def _(c):
                span = pl.ds(pl.multiple_of(c * CHUNK, CHUNK), CHUNK)
                parts, norm = centred([halo[side, n, span, :] for n in range(1, 4)])
                source_out[pl.ds(first + c * CHUNK, CHUNK)] = by_leaf(source_terms(parts, norm)).astype(BF16)

    charge_out[0:LEAVES] = halo[0, 0]
    charge_out[2 * LEAVES : 3 * LEAVES] = halo[1, 0]

    pl.loop(early, chunks)(far_chunk)

    finish_stage(2)
    every_out[...] = every[...]

    for stage in range(len(STAGES)):
        for k in range(1, STAGES[stage][1]):
            every_copy(stage, k).wait_send()
    for copy in sum(copies_of_halo, []) + moments:
        copy.wait_send()


def local_kernel(
    source, target, charges, every, pairs_vmem, bases, transfer, near_first, far_total,
    cluster_target_hbm, group_target_hbm, top_target_hbm, cluster_transfer_hbm, cluster_coupling_hbm,
    group_coupling_hbm, group_transfer_hbm, top_coupling_hbm,
    out, near_total,
    parts, cluster_transfer, cluster_coupling, group_coupling, group_transfer, top_coupling,
    group_moments, top_moments, pairs, cluster_target, group_target, top_target,
    sems,
):
    gx = lax.axis_index("gx")
    top = gx // 4

    loads = [
        pltpu.make_async_copy(source_ref, landing, sems.at[n])
        for n, (source_ref, landing) in enumerate(
            (
                (pairs_vmem, pairs),
                (cluster_target_hbm, cluster_target),
                (group_target_hbm, group_target),
                (top_target_hbm, top_target),
                (cluster_transfer_hbm, cluster_transfer),
                (cluster_coupling_hbm, cluster_coupling),
                (group_coupling_hbm, group_coupling),
                (group_transfer_hbm, group_transfer),
                (top_coupling_hbm.at[top], top_coupling),
            )
        )
    ]
    for copy in loads:
        copy.start()

    for k in range(GROUP):
        parts[k] = jnp.zeros((POINTS, 128), F32)
    loads[0].wait()

    def add_parts(g):
        for k in range(GROUP):
            near_total[pairs[0, g * GROUP + k] // 256] += parts[k]

    def listed_group(g):
        add_parts(jnp.maximum(g - 1, 0))
        for k in range(GROUP):
            code = pairs[0, g * GROUP + k]
            i, j = code // 256, code % 256
            square = jnp.dot(target[i], source[j], preferred_element_type=F32)
            parts[k] = folded(square, charges[pl.ds(j, 1), :])

    groups = (pairs[1, 0] + GROUP - 1) // GROUP

    @pl.loop(0, groups)
    def _(g):
        listed_group(g)

    add_parts(jnp.maximum(groups - 1, 0))

    unit = eye()
    for copy in loads[1:]:
        copy.wait()

    for g in range(32):
        group_moments[g : g + 1] = (
            every[4 * g, :, RANK:] + every[4 * g + 1, :, RANK:] + every[4 * g + 2, :, RANK:] + every[4 * g + 3, :, RANK:]
        )
    for h in range(8):
        total = jnp.zeros((RANK, RANK), F32)
        for k in range(4):
            g = 4 * h + k
            total = total + group_transfer[g] * to_column(group_moments[g : g + 1], unit)
        top_moments[h : h + 1] = jnp.sum(total, axis=0, keepdims=True)

    def masked(t):
        return jnp.where(t >= 0, 1.0, 0.0).astype(F32), jnp.maximum(t, 0)

    total = jnp.zeros((RANK, RANK), F32)
    for f in range(4):
        weight, t = masked(top_target[f, top])
        total = total + top_coupling[f] * (top_moments[pl.ds(t, 1), :] * weight)
    top_local = to_row(jnp.sum(total, axis=1, keepdims=True), unit)
    total = group_transfer[gx] * top_local
    for f in range(8):
        weight, t = masked(group_target[0, f])
        total = total + group_coupling[0, f] * (group_moments[pl.ds(t, 1), :] * weight)
    group_local = to_row(jnp.sum(total, axis=1, keepdims=True), unit)
    total = cluster_transfer[0] * group_local
    for f in range(8):
        weight, t = masked(cluster_target[0, f])
        total = total + cluster_coupling[0, f] * (every[t, :, :RANK] * weight)
    cluster_local = to_row(jnp.sum(total, axis=1, keepdims=True), unit)

    @pl.loop(0, LEAVES // CHUNK)
    def _(c):
        rows = []
        for k in range(CHUNK):
            i = c * CHUNK + k
            total = transfer[i] * cluster_local + far_total[i]
            leaf_local = jnp.sum(total, axis=1, keepdims=True)
            rows.append(jnp.sum(bases[i] * leaf_local, axis=0, keepdims=True))
        near_part = lane_sums(near_total.at[pl.ds(c * CHUNK, CHUNK)])
        out[pl.ds(pl.multiple_of(c * CHUNK, CHUNK), CHUNK), :] = near_part * INVERSE_FOUR_PI + jnp.concatenate(
            rows, axis=0
        )


def local(
    charges, points, leaf_bases, leaf_transfer, near_target, far_target, leaf_coupling, cluster_transfer,
    cluster_target, cluster_coupling, group_transfer, group_target, group_coupling, top_target, top_coupling,
):
    vmem = pl.BlockSpec(memory_space=pltpu.VMEM)
    anywhere = pl.BlockSpec(memory_space=pl.ANY)
    dma = pltpu.SemaphoreType.DMA

    def in_hbm(*arrays):
        return [pltpu.with_memory_space_constraint(array, pltpu.HBM) for array in arrays]

    handed = pl.pallas_call(
        exchange_kernel,
        out_shape=(
            pltpu.VMEM((3 * LEAVES + 1, TERMS, POINTS), BF16),
            pltpu.VMEM((LEAVES, POINTS, TERMS), BF16),
            pltpu.VMEM((3 * LEAVES + 8, POINTS), F32),
            pltpu.VMEM((DEVICES, 1, 2 * RANK), F32),
            pltpu.VMEM((2, PAIRS + 128), jnp.int32),
            pltpu.VMEM((LEAVES, RANK, POINTS), F32),
            pltpu.VMEM((LEAVES, RANK, RANK), F32),
            pltpu.VMEM((LEAVES, POINTS, 128), F32),
            pltpu.VMEM((LEAVES, RANK, RANK), F32),
        ),
        in_specs=[anywhere] * 8,
        out_specs=[vmem] * 9,
        scratch_shapes=[
            pltpu.VMEM((LEAVES * FAR, RANK, RANK), F32),
            pltpu.VMEM((LEAVES, FAR), jnp.int32),
            pltpu.SMEM((LEAVES, FAR), jnp.int32),
            pltpu.VMEM((5 * LEAVES + 8, RANK), F32),
            pltpu.VMEM((8, 128), jnp.int32),
            pltpu.SMEM((8, 128), jnp.int32),
            pltpu.VMEM((4, LEAVES, POINTS), F32),
            pltpu.VMEM((NEAR, LEAVES), jnp.int32),
            pltpu.VMEM((FAR, LEAVES), jnp.int32),
            pltpu.VMEM((1, RANK, RANK), F32),
            pltpu.VMEM((2, 4, LEAVES, POINTS), F32),
            pltpu.VMEM((5, LEAVES // 2, 2 * RANK), F32),
            pltpu.VMEM((DEVICES, 1, 2 * RANK), F32),
            dma((LEAVES // CHUNK,)),
            dma,
            dma,
            dma((2, LEAVES // CHUNK)),
            dma((5,)),
            dma((HALO_PARTS, 2)),
            dma((HALO_PARTS, 2)),
            dma((4,)),
            dma((4,)),
            dma((len(STAGES), 8)),
            dma((len(STAGES), 8)),
        ],
        compiler_params=pltpu.CompilerParams(
            collective_id=0, has_side_effects=True, vmem_limit_bytes=36 << 20
        ),
        name="exchange",
    )(
        *in_hbm(
            charges,
            jnp.transpose(points, (1, 0, 2)),
            near_target.T,
            far_target.T,
            cluster_transfer,
            jnp.swapaxes(leaf_bases, 1, 2),
            leaf_transfer,
            leaf_coupling.reshape(LEAVES * FAR, RANK, RANK),
        )
    )
    return pl.pallas_call(
        local_kernel,
        out_shape=(jax.ShapeDtypeStruct((LEAVES, POINTS), F32), pltpu.VMEM((LEAVES, POINTS, 128), F32)),
        in_specs=[vmem] * 9 + [anywhere] * 8,
        out_specs=[vmem] * 2,
        input_output_aliases={7: 1},
        scratch_shapes=[
            pltpu.VMEM((GROUP, POINTS, 128), F32),
            pltpu.VMEM((1, RANK, RANK), F32),
            pltpu.VMEM((1, 8, RANK, RANK), F32),
            pltpu.VMEM((1, 8, RANK, RANK), F32),
            pltpu.VMEM((32, RANK, RANK), F32),
            pltpu.VMEM((4, RANK, RANK), F32),
            pltpu.VMEM((32, RANK), F32),
            pltpu.VMEM((8, RANK), F32),
            pltpu.SMEM((2, PAIRS + 128), jnp.int32),
            pltpu.SMEM((1, 8), jnp.int32),
            pltpu.SMEM((1, 8), jnp.int32),
            pltpu.SMEM((4, 8), jnp.int32),
            dma((9,)),
        ],
        compiler_params=pltpu.CompilerParams(vmem_limit_bytes=36 << 20),
        name="local",
    )(
        *[pltpu.with_memory_space_constraint(array, pltpu.VMEM) for array in handed],
        *in_hbm(
            cluster_target,
            group_target,
            top_target.T,
            cluster_transfer,
            cluster_coupling,
            group_coupling,
            group_transfer,
            top_coupling,
        ),
    )[0]


def solution(mesh):
    leaf = ("gx", "gy")
    return jax.shard_map(
        local,
        mesh=mesh,
        in_specs=(
            P(leaf, None),
            P(leaf, None, None),
            P(leaf, None, None),
            P(leaf, None, None),
            P(leaf, None),
            P(leaf, None),
            P(leaf, None, None, None),
            P(leaf, None, None),
            P(leaf, None),
            P(leaf, None, None, None),
            P(),
            P("gx", None),
            P("gx", None, None, None),
            P(),
            P(),
        ),
        out_specs=P(leaf, None),
        check_vma=False,
    )
```

time: 52.6 us -> 43.7 us (0.83)
  the two profiles are of different devices: /device:TPU:1 before, /device:TPU:4 now
where the time goes in v3:
time: 43.7 us; the launch traced here: 43.6 us
  Pallas kernels  43.6 us (100%)
    pallas_call x1, Pallas kernels, local(): pl.pallas_call(exchange_kernel, out_shape=(pltpu.VMEM((3 * LEAVES + 1, TE...  25 us
    pallas_call x1, Pallas kernels, local(): pl.pallas_call(local_kernel, out_shape=(jax.ShapeDtypeStruct((LEAVES, POI...  18.6 us

profile of v3, /device:TPU:4, one launch (start us, length us, event | category | flops | bytes accessed | tf_op | source)
XLA Modules:
  0.0 43.6 jit_solution(15077928770104703201)
XLA Ops:
  0.0 25.0 %exchange.1 = (bf16[193,32,256]{2,1,0:T(8,128)(2,1)S(1)}, bf16[64,256,32]{2,1,0:T(8,128)(2,1)S(1)}, f32[200,256]{1,0:T(8,128)S(1)}, f32[128,1,128]{2,1,0:T(1,128...) custom-call(f32[64,256]{1,0:T(8,128)} %charges_hbm.1, ...), custom_call_target="tpu_custom_call" | custom-call | tf_op jit(solution)/shard_map/exchange/pallas_call | solution.py:498
  25.0 18.6 %local.1 = (f32[64,256]{1,0:T(8,128)}, f32[64,256,128]{2,1,0:T(8,128)S(1)}) custom-call(bf16[193,32,256]{2,1,0:T(8,128)(2,1)S(1)} %get-tuple-element.15.source, bf16[64,256,32]{2,1,0:T(8,128)(2,1)S(1)} %get-tuple-element.16.target, f32[200,256]{1,0:T(8,128)S(1)} %get-tuple-element.17.charges, ...), custom_call_target="tpu_custom_call", output_to_operand_aliasing={{1}: (7, {})} | custom-call | tf_op jit(solution)/shard_map/local/pallas_call | solution.py:555

commit v4 on v3

--- a/solution.py
+++ b/solution.py
@@ -22,10 +22,10 @@
 TERMS = 32
 PAIRS = LEAVES * NEAR
 GROUP = 16
-OWN = 1
+OWN = 2
 CHUNK = 8
 DEVICES = 128
-STAGES = ((1, 4), (4, 4), (16, 8))
+STAGES = ((1, 8), (8, 4), (32, 4))
 HALO_PARTS = 2
 BLANK = 3 * LEAVES
 
@@ -79,17 +79,16 @@
     return jnp.sum(unit * column, axis=0, keepdims=True)
 
 
-def merged(first, second, distance):
-    lane = lax.broadcasted_iota(jnp.int32, first.shape, 1)
-    here = (lane & distance) == 0
-    return jnp.where(here, first, second) + pltpu.roll(jnp.where(here, second, first), 128 - distance, axis=1)
-
-
 def lane_sums(parts):
-    parts = [parts[k] for k in range(CHUNK)]
-    for distance in (1, 2, 4):
-        parts = [merged(parts[n], parts[n + 1], distance) for n in range(0, len(parts), 2)]
-    return jnp.sum(parts[0].T.reshape(128 // CHUNK, CHUNK, POINTS), axis=0)
+    lane = lax.broadcasted_iota(jnp.int32, (128, 128), 1)
+    total = jnp.zeros((POINTS, 128), F32)
+    for k in range(0, CHUNK, 2):
+        ones = jnp.concatenate([jnp.where(lane == k + n, 1.0, 0.0) for n in range(2)], axis=0).astype(BF16)
+        pair = jnp.concatenate([parts[k], parts[k + 1]], axis=1)
+        high = pair.astype(BF16)
+        low = (pair - high.astype(F32)).astype(BF16)
+        total = total + jnp.dot(high, ones, preferred_element_type=F32) + jnp.dot(low, ones, preferred_element_type=F32)
+    return total.T[:CHUNK]
 
 
 def folded(square, charge):
@@ -153,10 +152,13 @@
     for distance in (1, -1, 2, -2):
         pl.semaphore_signal(barrier, inc=1, device_id=beside(distance), device_id_type=MESH)
 
+    row = gy * (DEVICES // 4) + gx
+
     def mate(stage, k):
         unit, count = STAGES[stage]
-        position = (device // unit) % count
-        return place(device + ((position + k) % count - position) * unit)
+        position = (row // unit) % count
+        there = row + ((position + k) % count - position) * unit
+        return (there % (DEVICES // 4), there // (DEVICES // 4))
 
     for stage in range(len(STAGES)):
 
@@ -227,9 +229,8 @@
         ]
         for part in range(HALO_PARTS)
     ]
-    for copies in copies_of_halo:
-        for copy in copies:
-            copy.start()
+    for copy in copies_of_halo[0]:
+        copy.start()
 
     lane = lax.broadcasted_iota(jnp.int32, (RANK, LEAVES), 1)
 
@@ -253,12 +254,12 @@
     unit = eye()
     cluster_row = jnp.sum(total, axis=0, keepdims=True)
     lifted_row = jnp.sum(cluster_transfer[0] * to_column(cluster_row, unit), axis=0, keepdims=True)
-    every[device, 0:1, 0:RANK] = cluster_row
-    every[device, 0:1, RANK : 2 * RANK] = lifted_row
+    every[row, 0:1, 0:RANK] = cluster_row
+    every[row, 0:1, RANK : 2 * RANK] = lifted_row
 
     def every_copy(stage, k):
         unit, _ = STAGES[stage]
-        rows = pl.ds((device // unit) * unit, unit)
+        rows = pl.ds((row // unit) * unit, unit)
         return pltpu.make_async_remote_copy(
             src_ref=every.at[rows],
             dst_ref=every.at[rows],
@@ -297,6 +298,9 @@
     moments = moment_copies()
     for copy in moments:
         copy.start()
+    for copies in copies_of_halo[1:]:
+        for copy in copies:
+            copy.start()
 
     @pl.loop(0, chunks)
     def _(c):
@@ -317,11 +321,12 @@
 
     choice_copy.wait()
 
-    @pl.loop(0, LEAVES // GROUP)
-    def _(g):
-        for k in range(GROUP):
-            i = g * GROUP + k
-            for n in range(OWN):
+    for n in range(OWN):
+
+        @pl.loop(0, LEAVES // GROUP)
+        def _(g):
+            for k in range(GROUP):
+                i = g * GROUP + k
                 j = jnp.clip(choice[n, i], 0, BLANK)
                 square = jnp.dot(target_out[i], source_out[j], preferred_element_type=F32)
                 part = folded(square, charge_out[pl.ds(j, 1), :])
@@ -330,8 +335,9 @@
                 else:
                     near_out[i] += part
 
-    finish_stage(1)
-    start_stage(2)
+        if n == 0:
+            finish_stage(1)
+            start_stage(2)
 
     for copy in moments:
         copy.wait_recv()
@@ -347,8 +353,8 @@
             i = c * CHUNK + k
             total = None
             for f in range(FAR):
-                row = jnp.clip(far_rows[i, f], 0, 5 * LEAVES)
-                term = coupling[i * FAR + f] * moment_rows[pl.ds(row, 1), :]
+                slot = jnp.clip(far_rows[i, f], 0, 5 * LEAVES)
+                term = coupling[i * FAR + f] * moment_rows[pl.ds(slot, 1), :]
                 total = term if total is None else total + term
             far_out[i] = total
 
@@ -387,7 +393,7 @@
     group_coupling_hbm, group_transfer_hbm, top_coupling_hbm,
     out, near_total,
     parts, cluster_transfer, cluster_coupling, group_coupling, group_transfer, top_coupling,
-    group_moments, top_moments, pairs, cluster_target, group_target, top_target,
+    group_moments, pairs, cluster_target, group_target, top_target,
     sems,
 ):
     gx = lax.axis_index("gx")
@@ -440,24 +446,19 @@
     for copy in loads[1:]:
         copy.wait()
 
-    for g in range(32):
-        group_moments[g : g + 1] = (
-            every[4 * g, :, RANK:] + every[4 * g + 1, :, RANK:] + every[4 * g + 2, :, RANK:] + every[4 * g + 3, :, RANK:]
-        )
-    for h in range(8):
-        total = jnp.zeros((RANK, RANK), F32)
-        for k in range(4):
-            g = 4 * h + k
-            total = total + group_transfer[g] * to_column(group_moments[g : g + 1], unit)
-        top_moments[h : h + 1] = jnp.sum(total, axis=0, keepdims=True)
-
+    quarter = DEVICES // 4
+    group_moments[...] = sum(every[pl.ds(k * quarter, quarter), 0, :][:, RANK:] for k in range(4))
     def masked(t):
         return jnp.where(t >= 0, 1.0, 0.0).astype(F32), jnp.maximum(t, 0)
 
     total = jnp.zeros((RANK, RANK), F32)
     for f in range(4):
         weight, t = masked(top_target[f, top])
-        total = total + top_coupling[f] * (top_moments[pl.ds(t, 1), :] * weight)
+        lifted = jnp.zeros((RANK, RANK), F32)
+        for k in range(4):
+            g = 4 * t + k
+            lifted = lifted + group_transfer[g] * to_column(group_moments[pl.ds(g, 1), :], unit)
+        total = total + top_coupling[f] * (jnp.sum(lifted, axis=0, keepdims=True) * weight)
     top_local = to_row(jnp.sum(total, axis=1, keepdims=True), unit)
     total = group_transfer[gx] * top_local
     for f in range(8):
@@ -467,7 +468,7 @@
     total = cluster_transfer[0] * group_local
     for f in range(8):
         weight, t = masked(cluster_target[0, f])
-        total = total + cluster_coupling[0, f] * (every[t, :, :RANK] * weight)
+        total = total + cluster_coupling[0, f] * (every[(t % 4) * quarter + t // 4, :, :RANK] * weight)
     cluster_local = to_row(jnp.sum(total, axis=1, keepdims=True), unit)
 
     @pl.loop(0, LEAVES // CHUNK)
@@ -566,7 +567,6 @@
             pltpu.VMEM((32, RANK, RANK), F32),
             pltpu.VMEM((4, RANK, RANK), F32),
             pltpu.VMEM((32, RANK), F32),
-            pltpu.VMEM((8, RANK), F32),
             pltpu.SMEM((2, PAIRS + 128), jnp.int32),
             pltpu.SMEM((1, 8), jnp.int32),
             pltpu.SMEM((1, 8), jnp.int32),

time: 43.7 us -> 38.9 us (0.89)
  the two profiles are of different devices: /device:TPU:4 before, /device:TPU:1 now
where the time goes in v4:
time: 38.9 us; the launch traced here: 38.8 us
  Pallas kernels  38.8 us (100%)
    pallas_call x1, Pallas kernels, local(): pl.pallas_call(exchange_kernel, out_shape=(pltpu.VMEM((3 * LEAVES + 1, TE...  22.8 us
    pallas_call x1, Pallas kernels, local(): pl.pallas_call(local_kernel, out_shape=(jax.ShapeDtypeStruct((LEAVES, POI...  16 us

profile of v4, /device:TPU:1, one launch (start us, length us, event | category | flops | bytes accessed | tf_op | source)
XLA Modules:
  0.0 38.8 jit_solution(14401400777478971)
XLA Ops:
  0.0 22.8 %exchange.1 = (bf16[193,32,256]{2,1,0:T(8,128)(2,1)S(1)}, bf16[64,256,32]{2,1,0:T(8,128)(2,1)S(1)}, f32[200,256]{1,0:T(8,128)S(1)}, f32[128,1,128]{2,1,0:T(1,128...) custom-call(f32[64,256]{1,0:T(8,128)} %charges_hbm.1, ...), custom_call_target="tpu_custom_call" | custom-call | tf_op jit(solution)/shard_map/exchange/pallas_call | solution.py:499
  22.8 16.0 %local.1 = (f32[64,256]{1,0:T(8,128)}, f32[64,256,128]{2,1,0:T(8,128)S(1)}) custom-call(bf16[193,32,256]{2,1,0:T(8,128)(2,1)S(1)} %get-tuple-element.15.source, bf16[64,256,32]{2,1,0:T(8,128)(2,1)S(1)} %get-tuple-element.16.target, f32[200,256]{1,0:T(8,128)S(1)} %get-tuple-element.17.charges, ...), custom_call_target="tpu_custom_call", output_to_operand_aliasing={{1}: (7, {})} | custom-call | tf_op jit(solution)/shard_map/local/pallas_call | solution.py:556

commit v5 on v4

--- a/solution.py
+++ b/solution.py
@@ -79,16 +79,24 @@
     return jnp.sum(unit * column, axis=0, keepdims=True)
 
 
-def lane_sums(parts):
-    lane = lax.broadcasted_iota(jnp.int32, (128, 128), 1)
-    total = jnp.zeros((POINTS, 128), F32)
-    for k in range(0, CHUNK, 2):
-        ones = jnp.concatenate([jnp.where(lane == k + n, 1.0, 0.0) for n in range(2)], axis=0).astype(BF16)
-        pair = jnp.concatenate([parts[k], parts[k + 1]], axis=1)
-        high = pair.astype(BF16)
-        low = (pair - high.astype(F32)).astype(BF16)
-        total = total + jnp.dot(high, ones, preferred_element_type=F32) + jnp.dot(low, ones, preferred_element_type=F32)
-    return total.T[:CHUNK]
+def lane_sums(parts, first):
+    odd = lax.broadcasted_iota(jnp.int32, (POINTS, 128), 1) % 2
+    source = lax.broadcasted_iota(jnp.int32, (256, 128), 0)
+    column = lax.broadcasted_iota(jnp.int32, (256, 128), 1) - first
+    total = None
+    for k in range(0, CHUNK, 4):
+        halves = []
+        for n in (k, k + 2):
+            here, there = parts[n], parts[n + 1]
+            halves.append(jnp.where(odd == 0, here, there) + pltpu.roll(jnp.where(odd == 0, there, here), 127, axis=1))
+        values = jnp.concatenate(halves, axis=1)
+        high = values.astype(BF16)
+        low = (values - high.astype(F32)).astype(BF16)
+        ones = jnp.where(k + source // 128 * 2 + source % 2 == column, 1.0, 0.0).astype(BF16)
+        for piece in (high, low):
+            term = jnp.dot(piece, ones, preferred_element_type=F32)
+            total = term if total is None else total + term
+    return total
 
 
 def folded(square, charge):
@@ -212,6 +220,20 @@
     pair_out[0:1, 0:PAIRS] = jnp.where(position_row < start, pairs, float(BLANK)).astype(jnp.int32)
     pair_out[0:1, PAIRS:] = jnp.full((1, 128), BLANK, jnp.int32)
     pair_out[1:2, 0:128] = jnp.broadcast_to(start.astype(jnp.int32), (1, 128))
+    @pl.loop(0, chunks)
+    def _(c):
+        span = pl.ds(pl.multiple_of(c * CHUNK, CHUNK), CHUNK)
+        parts, norm = centred([own[n, span, :] for n in range(1, 4)])
+        source_out[pl.ds(LEAVES + c * CHUNK, CHUNK)] = by_leaf(source_terms(parts, norm)).astype(BF16)
+        target = by_leaf(target_terms(parts, norm)).astype(BF16)
+        for k in range(CHUNK):
+            target_out[c * CHUNK + k] = target[k].T
+
+    charge_out[LEAVES : 2 * LEAVES] = own[0]
+    charge_out[3 * LEAVES :] = jnp.zeros((8, POINTS), F32)
+    term = lax.broadcasted_iota(jnp.int32, (TERMS, POINTS), 0)
+    source_out[BLANK] = jnp.where(term == 18, 1.0, 0.0).astype(BF16)
+
     pl.semaphore_wait(barrier, 4 + sum(count - 1 for _, count in STAGES))
 
     part_leaves = LEAVES // HALO_PARTS
@@ -302,23 +324,6 @@
         for copy in copies:
             copy.start()
 
-    @pl.loop(0, chunks)
-    def _(c):
-        span = pl.ds(pl.multiple_of(c * CHUNK, CHUNK), CHUNK)
-        parts, norm = centred([own[n, span, :] for n in range(1, 4)])
-        source_out[pl.ds(LEAVES + c * CHUNK, CHUNK)] = by_leaf(source_terms(parts, norm)).astype(BF16)
-        target = by_leaf(target_terms(parts, norm))
-        for k in range(CHUNK):
-            target_out[c * CHUNK + k] = target[k].T.astype(BF16)
-
-    charge_out[LEAVES : 2 * LEAVES] = own[0]
-    charge_out[3 * LEAVES :] = jnp.zeros((8, POINTS), F32)
-    term = lax.broadcasted_iota(jnp.int32, (TERMS, POINTS), 0)
-    source_out[BLANK] = jnp.where(term == 18, 1.0, 0.0).astype(BF16)
-
-    finish_stage(0)
-    start_stage(1)
-
     choice_copy.wait()
 
     for n in range(OWN):
@@ -336,8 +341,11 @@
                     near_out[i] += part
 
         if n == 0:
-            finish_stage(1)
-            start_stage(2)
+            finish_stage(0)
+            start_stage(1)
+
+    finish_stage(1)
+    start_stage(2)
 
     for copy in moments:
         copy.wait_recv()
@@ -392,7 +400,7 @@
     cluster_target_hbm, group_target_hbm, top_target_hbm, cluster_transfer_hbm, cluster_coupling_hbm,
     group_coupling_hbm, group_transfer_hbm, top_coupling_hbm,
     out, near_total,
-    parts, cluster_transfer, cluster_coupling, group_coupling, group_transfer, top_coupling,
+    parts, near_columns, cluster_transfer, cluster_coupling, group_coupling, group_transfer, top_coupling,
     group_moments, pairs, cluster_target, group_target, top_target,
     sems,
 ):
@@ -471,6 +479,8 @@
         total = total + cluster_coupling[0, f] * (every[(t % 4) * quarter + t // 4, :, :RANK] * weight)
     cluster_local = to_row(jnp.sum(total, axis=1, keepdims=True), unit)
 
+    near_columns[...] = jnp.zeros((POINTS, 128), F32)
+
     @pl.loop(0, LEAVES // CHUNK)
     def _(c):
         rows = []
@@ -479,10 +489,10 @@
             total = transfer[i] * cluster_local + far_total[i]
             leaf_local = jnp.sum(total, axis=1, keepdims=True)
             rows.append(jnp.sum(bases[i] * leaf_local, axis=0, keepdims=True))
-        near_part = lane_sums(near_total.at[pl.ds(c * CHUNK, CHUNK)])
-        out[pl.ds(pl.multiple_of(c * CHUNK, CHUNK), CHUNK), :] = near_part * INVERSE_FOUR_PI + jnp.concatenate(
-            rows, axis=0
-        )
+        near_columns[...] += lane_sums(near_total.at[pl.ds(c * CHUNK, CHUNK)], c * CHUNK)
+        out[pl.ds(pl.multiple_of(c * CHUNK, CHUNK), CHUNK), :] = jnp.concatenate(rows, axis=0)
+
+    out[...] += near_columns[...].T[:LEAVES] * INVERSE_FOUR_PI
 
 
 def local(
@@ -561,6 +571,7 @@
         input_output_aliases={7: 1},
         scratch_shapes=[
             pltpu.VMEM((GROUP, POINTS, 128), F32),
+            pltpu.VMEM((POINTS, 128), F32),
             pltpu.VMEM((1, RANK, RANK), F32),
             pltpu.VMEM((1, 8, RANK, RANK), F32),
             pltpu.VMEM((1, 8, RANK, RANK), F32),

time: 38.9 us -> 35.9 us (0.923)
  the two profiles are of different devices: /device:TPU:1 before, /device:TPU:0 now
where the time goes in v5:
time: 35.9 us; the launch traced here: 35.8 us
  Pallas kernels  35.8 us (100%)
    pallas_call x1, Pallas kernels, local(): pl.pallas_call(exchange_kernel, out_shape=(pltpu.VMEM((3 * LEAVES + 1, TE...  21.4 us
    pallas_call x1, Pallas kernels, local(): pl.pallas_call(local_kernel, out_shape=(jax.ShapeDtypeStruct((LEAVES, POI...  14.4 us

profile of v5, /device:TPU:0, one launch (start us, length us, event | category | flops | bytes accessed | tf_op | source)
XLA Modules:
  0.0 35.8 jit_solution(17990784109707928486)
XLA Ops:
  0.0 21.4 %exchange.1 = (bf16[193,32,256]{2,1,0:T(8,128)(2,1)S(1)}, bf16[64,256,32]{2,1,0:T(8,128)(2,1)S(1)}, f32[200,256]{1,0:T(8,128)S(1)}, f32[128,1,128]{2,1,0:T(1,128...) custom-call(f32[64,256]{1,0:T(8,128)} %charges_hbm.1, ...), custom_call_target="tpu_custom_call" | custom-call | tf_op jit(solution)/shard_map/exchange/pallas_call | solution.py:509
  21.4 14.4 %local.1 = (f32[64,256]{1,0:T(8,128)}, f32[64,256,128]{2,1,0:T(8,128)S(1)}) custom-call(bf16[193,32,256]{2,1,0:T(8,128)(2,1)S(1)} %get-tuple-element.15.source, bf16[64,256,32]{2,1,0:T(8,128)(2,1)S(1)} %get-tuple-element.16.target, f32[200,256]{1,0:T(8,128)S(1)} %get-tuple-element.17.charges, ...), custom_call_target="tpu_custom_call", output_to_operand_aliasing={{1}: (7, {})} | custom-call | tf_op jit(solution)/shard_map/local/pallas_call | solution.py:566

commit v6 on v5

--- a/solution.py
+++ b/solution.py
@@ -120,6 +120,9 @@
         return place((device + distance + DEVICES) % DEVICES)
 
     chunks = LEAVES // CHUNK
+    lower = device < DEVICES // 2
+    sooner = jnp.where(lower, chunks, 0)
+    own_limit = jnp.where(lower, OWN, 1)
 
     def load_copies(c):
         span = pl.ds(c * CHUNK, CHUNK)
@@ -190,8 +193,8 @@
     for s in range(NEAR):
         is_own = is_here[s : s + 1] > 0
         for n in range(OWN):
-            chosen[n] = jnp.where(is_own & (own_before == n), local_slots[s : s + 1] + LEAVES, chosen[n])
-        left = jnp.where(is_own & (own_before < OWN), 0.0, 1.0)
+            chosen[n] = jnp.where(is_own & (own_before == n) & (n < own_limit), local_slots[s : s + 1] + LEAVES, chosen[n])
+        left = jnp.where(is_own & (own_before < own_limit), 0.0, 1.0)
         live_rows.append(jnp.where(slots[s : s + 1] >= 0, left, 0.0))
         own_before = own_before + is_here[s : s + 1]
     for n in range(OWN):
@@ -220,8 +223,7 @@
     pair_out[0:1, 0:PAIRS] = jnp.where(position_row < start, pairs, float(BLANK)).astype(jnp.int32)
     pair_out[0:1, PAIRS:] = jnp.full((1, 128), BLANK, jnp.int32)
     pair_out[1:2, 0:128] = jnp.broadcast_to(start.astype(jnp.int32), (1, 128))
-    @pl.loop(0, chunks)
-    def _(c):
+    def own_terms(c):
         span = pl.ds(pl.multiple_of(c * CHUNK, CHUNK), CHUNK)
         parts, norm = centred([own[n, span, :] for n in range(1, 4)])
         source_out[pl.ds(LEAVES + c * CHUNK, CHUNK)] = by_leaf(source_terms(parts, norm)).astype(BF16)
@@ -229,11 +231,29 @@
         for k in range(CHUNK):
             target_out[c * CHUNK + k] = target[k].T
 
+    pl.loop(0, sooner)(own_terms)
     charge_out[LEAVES : 2 * LEAVES] = own[0]
     charge_out[3 * LEAVES :] = jnp.zeros((8, POINTS), F32)
     term = lax.broadcasted_iota(jnp.int32, (TERMS, POINTS), 0)
     source_out[BLANK] = jnp.where(term == 18, 1.0, 0.0).astype(BF16)
 
+    lane = lax.broadcasted_iota(jnp.int32, (RANK, LEAVES), 1)
+
+    def moment_chunk(c, carry):
+        columns, total = carry
+        for copy in load_copies(c):
+            copy.wait()
+        weights = own[0, pl.ds(pl.multiple_of(c * CHUNK, CHUNK), CHUNK), :]
+        for k in range(CHUNK):
+            product = bases[c * CHUNK + k] * weights[k : k + 1, :]
+            column = jnp.sum(product[:, :128] + product[:, 128:], axis=1, keepdims=True)
+            columns = jnp.where(lane == c * CHUNK + k, column, columns)
+            total = total + transfer[c * CHUNK + k] * column
+        return columns, total
+
+    carry = lax.fori_loop(
+        0, sooner, moment_chunk, (jnp.zeros((RANK, LEAVES), F32), jnp.zeros((RANK, RANK), F32))
+    )
     pl.semaphore_wait(barrier, 4 + sum(count - 1 for _, count in STAGES))
 
     part_leaves = LEAVES // HALO_PARTS
@@ -254,23 +274,7 @@
     for copy in copies_of_halo[0]:
         copy.start()
 
-    lane = lax.broadcasted_iota(jnp.int32, (RANK, LEAVES), 1)
-
-    def moment_chunk(c, carry):
-        columns, total = carry
-        for copy in load_copies(c):
-            copy.wait()
-        weights = own[0, pl.ds(pl.multiple_of(c * CHUNK, CHUNK), CHUNK), :]
-        for k in range(CHUNK):
-            product = bases[c * CHUNK + k] * weights[k : k + 1, :]
-            column = jnp.sum(product[:, :128] + product[:, 128:], axis=1, keepdims=True)
-            columns = jnp.where(lane == c * CHUNK + k, column, columns)
-            total = total + transfer[c * CHUNK + k] * column
-        return columns, total
-
-    columns, total = lax.fori_loop(
-        0, chunks, moment_chunk, (jnp.zeros((RANK, LEAVES), F32), jnp.zeros((RANK, RANK), F32))
-    )
+    columns, total = lax.fori_loop(sooner, chunks, moment_chunk, carry)
     rows = columns.T
     window[2] = jnp.concatenate([rows[: LEAVES // 2], rows[LEAVES // 2 :]], axis=1)
     unit = eye()
@@ -324,11 +328,13 @@
         for copy in copies:
             copy.start()
 
+    pl.loop(sooner, chunks)(own_terms)
+
     choice_copy.wait()
 
     for n in range(OWN):
 
-        @pl.loop(0, LEAVES // GROUP)
+        @pl.loop(0, LEAVES // GROUP if n == 0 else jnp.where(lower, LEAVES // GROUP, 0))
         def _(g):
             for k in range(GROUP):
                 i = g * GROUP + k
@@ -340,12 +346,12 @@
                 else:
                     near_out[i] += part
 
-        if n == 0:
-            finish_stage(0)
-            start_stage(1)
-
-    finish_stage(1)
-    start_stage(2)
+            if n == 0:
+
+                @pl.when(g == 1)
+                def _():
+                    finish_stage(0)
+                    start_stage(1)
 
     for copy in moments:
         copy.wait_recv()
@@ -366,8 +372,13 @@
                 total = term if total is None else total + term
             far_out[i] = total
 
-    early = chunks * 5 // 8
-    pl.loop(0, early)(far_chunk)
+    def far_chunks(first, last):
+        pl.loop(first, last)(far_chunk)
+
+    far_chunks(0, 3)
+    finish_stage(1)
+    start_stage(2)
+    far_chunks(3, 5)
 
     for part in range(HALO_PARTS):
         for side in range(2):
@@ -383,7 +394,7 @@
     charge_out[0:LEAVES] = halo[0, 0]
     charge_out[2 * LEAVES : 3 * LEAVES] = halo[1, 0]
 
-    pl.loop(early, chunks)(far_chunk)
+    far_chunks(5, chunks)
 
     finish_stage(2)
     every_out[...] = every[...]

time: 35.9 us -> 36.9 us (1.028)
  the two profiles are of different devices: /device:TPU:0 before, /device:TPU:1 now
where the time goes in v6:
time: 36.9 us; the launch traced here: 36.6 us
  Pallas kernels  36.6 us (99%)
    pallas_call x1, Pallas kernels, local(): pl.pallas_call(exchange_kernel, out_shape=(pltpu.VMEM((3 * LEAVES + 1, TE...  22.2 us
    pallas_call x1, Pallas kernels, local(): pl.pallas_call(local_kernel, out_shape=(jax.ShapeDtypeStruct((LEAVES, POI...  14.4 us

profile of v6, /device:TPU:1, one launch (start us, length us, event | category | flops | bytes accessed | tf_op | source)
XLA Modules:
  0.0 36.6 jit_solution(5666031458974603533)
XLA Ops:
  0.0 22.2 %exchange.1 = (bf16[193,32,256]{2,1,0:T(8,128)(2,1)S(1)}, bf16[64,256,32]{2,1,0:T(8,128)(2,1)S(1)}, f32[200,256]{1,0:T(8,128)S(1)}, f32[128,1,128]{2,1,0:T(1,128...) custom-call(f32[64,256]{1,0:T(8,128)} %charges_hbm.1, ...), custom_call_target="tpu_custom_call" | custom-call | tf_op jit(solution)/shard_map/exchange/pallas_call | solution.py:520
  22.2 14.4 %local.1 = (f32[64,256]{1,0:T(8,128)}, f32[64,256,128]{2,1,0:T(8,128)S(1)}) custom-call(bf16[193,32,256]{2,1,0:T(8,128)(2,1)S(1)} %get-tuple-element.15.source, bf16[64,256,32]{2,1,0:T(8,128)(2,1)S(1)} %get-tuple-element.16.target, f32[200,256]{1,0:T(8,128)S(1)} %get-tuple-element.17.charges, ...), custom_call_target="tpu_custom_call", output_to_operand_aliasing={{1}: (7, {})} | custom-call | tf_op jit(solution)/shard_map/local/pallas_call | solution.py:577

commit v7 on v6

--- a/solution.py
+++ b/solution.py
@@ -21,7 +21,9 @@
 FAR = 16
 TERMS = 32
 PAIRS = LEAVES * NEAR
-GROUP = 16
+GROUP = 32
+LAST_GROUP = 16
+EXCHANGED = 48
 OWN = 2
 CHUNK = 8
 DEVICES = 128
@@ -106,8 +108,8 @@
 
 def exchange_kernel(
     charges_hbm, points_hbm, near_hbm, far_hbm, cluster_transfer_hbm, bases_hbm, transfer_hbm, coupling_hbm,
-    source_out, target_out, charge_out, every_out, pair_out, bases, transfer, near_out, far_out,
-    coupling, far_vector, far_rows, moment_rows, choice_vector, choice, own, near, far, cluster_transfer, halo, window, every,
+    source_out, target_out, charge_out, every_out, pair_out, bases, transfer, near_out, far_out, far_vector, moment_rows,
+    coupling, far_rows, choice_vector, choice, own, near, far, cluster_transfer, halo, window, every,
     coupling_sems, far_sem, choice_sem, load_sems, small_sems, halo_send, halo_recv, moment_send, moment_recv, every_send, every_recv,
 ):
     gx, gy = lax.axis_index("gx"), lax.axis_index("gy")
@@ -120,9 +122,10 @@
         return place((device + distance + DEVICES) % DEVICES)
 
     chunks = LEAVES // CHUNK
-    lower = device < DEVICES // 2
-    sooner = jnp.where(lower, chunks, 0)
-    own_limit = jnp.where(lower, OWN, 1)
+    lateness = (gx // 2) % 4 + gx // 8 + 2 * gy
+    terms_before = jnp.where(lateness <= 6, chunks, 0)
+    moments_before = jnp.where(lateness <= 4, chunks, 0)
+    own_limit = jnp.where(lateness <= 8, OWN, 1)
 
     def load_copies(c):
         span = pl.ds(c * CHUNK, CHUNK)
@@ -155,7 +158,9 @@
         span = pl.ds(c * CHUNK * FAR, CHUNK * FAR)
         return pltpu.make_async_copy(coupling_hbm.at[span], coupling.at[span], coupling_sems.at[c])
 
-    @pl.loop(0, chunks)
+    far_chunk_count = EXCHANGED // CHUNK
+
+    @pl.loop(0, far_chunk_count)
     def _(c):
         coupling_copy(c).start()
 
@@ -231,7 +236,7 @@
         for k in range(CHUNK):
             target_out[c * CHUNK + k] = target[k].T
 
-    pl.loop(0, sooner)(own_terms)
+    pl.loop(0, terms_before)(own_terms)
     charge_out[LEAVES : 2 * LEAVES] = own[0]
     charge_out[3 * LEAVES :] = jnp.zeros((8, POINTS), F32)
     term = lax.broadcasted_iota(jnp.int32, (TERMS, POINTS), 0)
@@ -252,7 +257,7 @@
         return columns, total
 
     carry = lax.fori_loop(
-        0, sooner, moment_chunk, (jnp.zeros((RANK, LEAVES), F32), jnp.zeros((RANK, RANK), F32))
+        0, moments_before, moment_chunk, (jnp.zeros((RANK, LEAVES), F32), jnp.zeros((RANK, RANK), F32))
     )
     pl.semaphore_wait(barrier, 4 + sum(count - 1 for _, count in STAGES))
 
@@ -274,7 +279,7 @@
     for copy in copies_of_halo[0]:
         copy.start()
 
-    columns, total = lax.fori_loop(sooner, chunks, moment_chunk, carry)
+    columns, total = lax.fori_loop(moments_before, chunks, moment_chunk, carry)
     rows = columns.T
     window[2] = jnp.concatenate([rows[: LEAVES // 2], rows[LEAVES // 2 :]], axis=1)
     unit = eye()
@@ -328,13 +333,13 @@
         for copy in copies:
             copy.start()
 
-    pl.loop(sooner, chunks)(own_terms)
+    pl.loop(terms_before, chunks)(own_terms)
 
     choice_copy.wait()
 
     for n in range(OWN):
 
-        @pl.loop(0, LEAVES // GROUP if n == 0 else jnp.where(lower, LEAVES // GROUP, 0))
+        @pl.loop(0, LEAVES // GROUP if n == 0 else jnp.where(own_limit > n, LEAVES // GROUP, 0))
         def _(g):
             for k in range(GROUP):
                 i = g * GROUP + k
@@ -348,7 +353,7 @@
 
             if n == 0:
 
-                @pl.when(g == 1)
+                @pl.when(g == 0)
                 def _():
                     finish_stage(0)
                     start_stage(1)
@@ -375,10 +380,10 @@
     def far_chunks(first, last):
         pl.loop(first, last)(far_chunk)
 
-    far_chunks(0, 3)
+    far_chunks(0, 2)
     finish_stage(1)
     start_stage(2)
-    far_chunks(3, 5)
+    far_chunks(2, 4)
 
     for part in range(HALO_PARTS):
         for side in range(2):
@@ -394,7 +399,7 @@
     charge_out[0:LEAVES] = halo[0, 0]
     charge_out[2 * LEAVES : 3 * LEAVES] = halo[1, 0]
 
-    far_chunks(5, chunks)
+    far_chunks(4, far_chunk_count)
 
     finish_stage(2)
     every_out[...] = every[...]
@@ -407,11 +412,11 @@
 
 
 def local_kernel(
-    source, target, charges, every, pairs_vmem, bases, transfer, near_first, far_total,
+    source, target, charges, every, pairs_vmem, bases, transfer, near_first, far_first, far_vmem, moments,
     cluster_target_hbm, group_target_hbm, top_target_hbm, cluster_transfer_hbm, cluster_coupling_hbm,
-    group_coupling_hbm, group_transfer_hbm, top_coupling_hbm,
-    out, near_total,
-    parts, near_columns, cluster_transfer, cluster_coupling, group_coupling, group_transfer, top_coupling,
+    group_coupling_hbm, group_transfer_hbm, top_coupling_hbm, coupling_hbm,
+    out, near_total, far_total,
+    coupling, far_rows, parts, near_columns, cluster_transfer, cluster_coupling, group_coupling, group_transfer, top_coupling,
     group_moments, pairs, cluster_target, group_target, top_target,
     sems,
 ):
@@ -423,6 +428,7 @@
         for n, (source_ref, landing) in enumerate(
             (
                 (pairs_vmem, pairs),
+                (far_vmem, far_rows),
                 (cluster_target_hbm, cluster_target),
                 (group_target_hbm, group_target),
                 (top_target_hbm, top_target),
@@ -431,6 +437,7 @@
                 (group_coupling_hbm, group_coupling),
                 (group_transfer_hbm, group_transfer),
                 (top_coupling_hbm.at[top], top_coupling),
+                (coupling_hbm.at[pl.ds(EXCHANGED * FAR, (LEAVES - EXCHANGED) * FAR)], coupling),
             )
         )
     ]
@@ -441,29 +448,46 @@
         parts[k] = jnp.zeros((POINTS, 128), F32)
     loads[0].wait()
 
-    def add_parts(g):
-        for k in range(GROUP):
-            near_total[pairs[0, g * GROUP + k] // 256] += parts[k]
-
-    def listed_group(g):
-        add_parts(jnp.maximum(g - 1, 0))
-        for k in range(GROUP):
-            code = pairs[0, g * GROUP + k]
+    def add_parts(first, count):
+        for k in range(count):
+            near_total[pairs[0, first + k] // 256] += parts[k]
+
+    def listed_pairs(first, count):
+        for k in range(count):
+            code = pairs[0, first + k]
             i, j = code // 256, code % 256
             square = jnp.dot(target[i], source[j], preferred_element_type=F32)
             parts[k] = folded(square, charges[pl.ds(j, 1), :])
 
-    groups = (pairs[1, 0] + GROUP - 1) // GROUP
+    live = pairs[1, 0]
+    groups = (live + GROUP - LAST_GROUP - 1) // GROUP
 
     @pl.loop(0, groups)
     def _(g):
-        listed_group(g)
-
-    add_parts(jnp.maximum(groups - 1, 0))
+        add_parts(jnp.maximum(g - 1, 0) * GROUP, GROUP)
+        listed_pairs(g * GROUP, GROUP)
+
+    add_parts(jnp.maximum(groups - 1, 0) * GROUP, GROUP)
+
+    @pl.when(live > groups * GROUP)
+    def _():
+        listed_pairs(groups * GROUP, LAST_GROUP)
+        add_parts(groups * GROUP, LAST_GROUP)
 
     unit = eye()
     for copy in loads[1:]:
         copy.wait()
+
+    @pl.loop(0, (LEAVES - EXCHANGED) // CHUNK)
+    def _(c):
+        for k in range(CHUNK):
+            i = c * CHUNK + k
+            total = None
+            for f in range(FAR):
+                term = coupling[i * FAR + f] * moments[pl.ds(far_rows[EXCHANGED + i, f], 1), :]
+                total = term if total is None else total + term
+            far_total[EXCHANGED + i] = total
+
 
     quarter = DEVICES // 4
     group_moments[...] = sum(every[pl.ds(k * quarter, quarter), 0, :][:, RANK:] for k in range(4))
@@ -529,14 +553,14 @@
             pltpu.VMEM((LEAVES, RANK, RANK), F32),
             pltpu.VMEM((LEAVES, POINTS, 128), F32),
             pltpu.VMEM((LEAVES, RANK, RANK), F32),
+            pltpu.VMEM((LEAVES, FAR), jnp.int32),
+            pltpu.VMEM((5 * LEAVES + 8, RANK), F32),
         ),
         in_specs=[anywhere] * 8,
-        out_specs=[vmem] * 9,
+        out_specs=[vmem] * 11,
         scratch_shapes=[
-            pltpu.VMEM((LEAVES * FAR, RANK, RANK), F32),
-            pltpu.VMEM((LEAVES, FAR), jnp.int32),
+            pltpu.VMEM((EXCHANGED * FAR, RANK, RANK), F32),
             pltpu.SMEM((LEAVES, FAR), jnp.int32),
-            pltpu.VMEM((5 * LEAVES + 8, RANK), F32),
             pltpu.VMEM((8, 128), jnp.int32),
             pltpu.SMEM((8, 128), jnp.int32),
             pltpu.VMEM((4, LEAVES, POINTS), F32),
@@ -559,7 +583,7 @@
             dma((len(STAGES), 8)),
         ],
         compiler_params=pltpu.CompilerParams(
-            collective_id=0, has_side_effects=True, vmem_limit_bytes=36 << 20
+            collective_id=0, has_side_effects=True, vmem_limit_bytes=30 << 20
         ),
         name="exchange",
     )(
@@ -576,11 +600,17 @@
     )
     return pl.pallas_call(
         local_kernel,
-        out_shape=(jax.ShapeDtypeStruct((LEAVES, POINTS), F32), pltpu.VMEM((LEAVES, POINTS, 128), F32)),
-        in_specs=[vmem] * 9 + [anywhere] * 8,
-        out_specs=[vmem] * 2,
-        input_output_aliases={7: 1},
+        out_shape=(
+            jax.ShapeDtypeStruct((LEAVES, POINTS), F32),
+            pltpu.VMEM((LEAVES, POINTS, 128), F32),
+            pltpu.VMEM((LEAVES, RANK, RANK), F32),
+        ),
+        in_specs=[vmem] * 11 + [anywhere] * 9,
+        out_specs=[vmem] * 3,
+        input_output_aliases={7: 1, 8: 2},
         scratch_shapes=[
+            pltpu.VMEM(((LEAVES - EXCHANGED) * FAR, RANK, RANK), F32),
+            pltpu.SMEM((LEAVES, FAR), jnp.int32),
             pltpu.VMEM((GROUP, POINTS, 128), F32),
             pltpu.VMEM((POINTS, 128), F32),
             pltpu.VMEM((1, RANK, RANK), F32),
@@ -593,9 +623,9 @@
             pltpu.SMEM((1, 8), jnp.int32),
             pltpu.SMEM((1, 8), jnp.int32),
             pltpu.SMEM((4, 8), jnp.int32),
-            dma((9,)),
+            dma((11,)),
         ],
-        compiler_params=pltpu.CompilerParams(vmem_limit_bytes=36 << 20),
+        compiler_params=pltpu.CompilerParams(vmem_limit_bytes=30 << 20),
         name="local",
     )(
         *[pltpu.with_memory_space_constraint(array, pltpu.VMEM) for array in handed],
@@ -608,6 +638,7 @@
             group_coupling,
             group_transfer,
             top_coupling,
+            leaf_coupling.reshape(LEAVES * FAR, RANK, RANK),
         ),
     )[0]
 

time: 36.9 us -> 35.5 us (0.962)
  Pallas kernels: 36.6 us -> 35.2 us
    pallas_call x1, Pallas kernels: 22.2 us -> 20.9 us  [local(): pl.pallas_call(exchange_kernel, out_shape=(pltpu.VMEM((3 * LEAVES + 1, TE...]
where the time goes in v7:
time: 35.5 us; the launch traced here: 35.2 us
  Pallas kernels  35.2 us (99%)
    pallas_call x1, Pallas kernels, local(): pl.pallas_call(exchange_kernel, out_shape=(pltpu.VMEM((3 * LEAVES + 1, TE...  20.9 us
    pallas_call x1, Pallas kernels, local(): pl.pallas_call(local_kernel, out_shape=(jax.ShapeDtypeStruct((LEAVES, POI...  14.3 us

profile of v7, /device:TPU:1, one launch (start us, length us, event | category | flops | bytes accessed | tf_op | source)
XLA Modules:
  0.0 35.2 jit_solution(4698360201970236939)
XLA Ops:
  0.0 20.9 %exchange.1 = (bf16[193,32,256]{2,1,0:T(8,128)(2,1)S(1)}, bf16[64,256,32]{2,1,0:T(8,128)(2,1)S(1)}, f32[200,256]{1,0:T(8,128)S(1)}, f32[128,1,128]{2,1,0:T(1,128...) custom-call(f32[64,256]{1,0:T(8,128)} %charges_hbm.1, ...), custom_call_target="tpu_custom_call" | custom-call | tf_op jit(solution)/shard_map/exchange/pallas_call | solution.py:544
  20.9 14.3 %local.1 = (f32[64,256]{1,0:T(8,128)}, f32[64,256,128]{2,1,0:T(8,128)S(1)}, f32[64,64,64]{2,1,0:T(8,128)S(1)}) custom-call(bf16[193,32,256]{2,1,0:T(8,128)(2,1)S(1)} %get-tuple-element.17.source, bf16[64,256,32]{2,1,0:T(8,128)(2,1)S(1)} %get-tuple-element.18.target, ...), custom_call_target="tpu_custom_call", output_to_operand_aliasing={{1}: (7, {}), {2}: (8, {})} | custom-call | tf_op jit(solution)/shard_map/local/pallas_call | solution.py:601

commit v8 on v7

--- a/solution.py
+++ b/solution.py
@@ -125,7 +125,7 @@
     lateness = (gx // 2) % 4 + gx // 8 + 2 * gy
     terms_before = jnp.where(lateness <= 6, chunks, 0)
     moments_before = jnp.where(lateness <= 4, chunks, 0)
-    own_limit = jnp.where(lateness <= 8, OWN, 1)
+    own_limit = jnp.where(lateness <= 6, OWN, 1)
 
     def load_copies(c):
         span = pl.ds(c * CHUNK, CHUNK)
@@ -159,10 +159,6 @@
         return pltpu.make_async_copy(coupling_hbm.at[span], coupling.at[span], coupling_sems.at[c])
 
     far_chunk_count = EXCHANGED // CHUNK
-
-    @pl.loop(0, far_chunk_count)
-    def _(c):
-        coupling_copy(c).start()
 
     barrier = pltpu.get_barrier_semaphore()
     for distance in (1, -1, 2, -2):
@@ -310,6 +306,10 @@
 
     start_stage(0)
 
+    @pl.loop(0, far_chunk_count)
+    def _(c):
+        coupling_copy(c).start()
+
     def moment_copies():
         copies = []
         for n, distance in enumerate((2, 1, -1, -2)):
@@ -351,12 +351,15 @@
                 else:
                     near_out[i] += part
 
-            if n == 0:
-
-                @pl.when(g == 0)
-                def _():
-                    finish_stage(0)
-                    start_stage(1)
+            @pl.when(g == 0)
+            def _():
+                finish_stage(n)
+                start_stage(n + 1)
+
+    @pl.when(own_limit < 2)
+    def _():
+        finish_stage(1)
+        start_stage(2)
 
     for copy in moments:
         copy.wait_recv()
@@ -380,10 +383,7 @@
     def far_chunks(first, last):
         pl.loop(first, last)(far_chunk)
 
-    far_chunks(0, 2)
-    finish_stage(1)
-    start_stage(2)
-    far_chunks(2, 4)
+    far_chunks(0, 4)
 
     for part in range(HALO_PARTS):
         for side in range(2):
@@ -467,12 +467,17 @@
         add_parts(jnp.maximum(g - 1, 0) * GROUP, GROUP)
         listed_pairs(g * GROUP, GROUP)
 
-    add_parts(jnp.maximum(groups - 1, 0) * GROUP, GROUP)
+    last = jnp.maximum(groups - 1, 0) * GROUP
 
     @pl.when(live > groups * GROUP)
     def _():
+        add_parts(last, GROUP)
         listed_pairs(groups * GROUP, LAST_GROUP)
         add_parts(groups * GROUP, LAST_GROUP)
+
+    @pl.when(live <= groups * GROUP)
+    def _():
+        add_parts(last, GROUP)
 
     unit = eye()
     for copy in loads[1:]:

time: 35.5 us -> 35.5 us (level)
  no operation moved by 1% of the time
where the time goes in v8:
time: 35.5 us; the launch traced here: 34.9 us
  Pallas kernels  34.9 us (98%)
    pallas_call x1, Pallas kernels, local(): pl.pallas_call(exchange_kernel, out_shape=(pltpu.VMEM((3 * LEAVES + 1, TE...  20.6 us
    pallas_call x1, Pallas kernels, local(): pl.pallas_call(local_kernel, out_shape=(jax.ShapeDtypeStruct((LEAVES, POI...  14.3 us

profile of v8, /device:TPU:1, one launch (start us, length us, event | category | flops | bytes accessed | tf_op | source)
XLA Modules:
  0.0 34.9 jit_solution(4246174985808396088)
XLA Ops:
  0.0 20.6 %exchange.1 = (bf16[193,32,256]{2,1,0:T(8,128)(2,1)S(1)}, bf16[64,256,32]{2,1,0:T(8,128)(2,1)S(1)}, f32[200,256]{1,0:T(8,128)S(1)}, f32[128,1,128]{2,1,0:T(1,128...) custom-call(f32[64,256]{1,0:T(8,128)} %charges_hbm.1, ...), custom_call_target="tpu_custom_call" | custom-call | tf_op jit(solution)/shard_map/exchange/pallas_call | solution.py:549
  20.6 14.3 %local.1 = (f32[64,256]{1,0:T(8,128)}, f32[64,256,128]{2,1,0:T(8,128)S(1)}, f32[64,64,64]{2,1,0:T(8,128)S(1)}) custom-call(bf16[193,32,256]{2,1,0:T(8,128)(2,1)S(1)} %get-tuple-element.17.source, bf16[64,256,32]{2,1,0:T(8,128)(2,1)S(1)} %get-tuple-element.18.target, ...), custom_call_target="tpu_custom_call", output_to_operand_aliasing={{1}: (7, {}), {2}: (8, {})} | custom-call | tf_op jit(solution)/shard_map/local/pallas_call | solution.py:606

commit v9 on v8

--- a/solution.py
+++ b/solution.py
@@ -24,11 +24,11 @@
 GROUP = 32
 LAST_GROUP = 16
 EXCHANGED = 48
-OWN = 2
+OWN = 3
 CHUNK = 8
 DEVICES = 128
 STAGES = ((1, 8), (8, 4), (32, 4))
-HALO_PARTS = 2
+HALO_PARTS = 4
 BLANK = 3 * LEAVES
 
 
@@ -125,7 +125,7 @@
     lateness = (gx // 2) % 4 + gx // 8 + 2 * gy
     terms_before = jnp.where(lateness <= 6, chunks, 0)
     moments_before = jnp.where(lateness <= 4, chunks, 0)
-    own_limit = jnp.where(lateness <= 6, OWN, 1)
+    own_limit = jnp.where(lateness <= 3, OWN, jnp.where(lateness <= 6, 2, 1))
 
     def load_copies(c):
         span = pl.ds(c * CHUNK, CHUNK)
@@ -304,6 +304,12 @@
         for k in range(1, STAGES[stage][1]):
             every_copy(stage, k).wait_recv()
 
+    def next_stage(stage):
+        finish_stage(stage)
+        start_stage(stage + 1)
+        for copy in copies_of_halo[stage + 2]:
+            copy.start()
+
     start_stage(0)
 
     @pl.loop(0, far_chunk_count)
@@ -329,9 +335,8 @@
     moments = moment_copies()
     for copy in moments:
         copy.start()
-    for copies in copies_of_halo[1:]:
-        for copy in copies:
-            copy.start()
+    for copy in copies_of_halo[1]:
+        copy.start()
 
     pl.loop(terms_before, chunks)(own_terms)
 
@@ -351,15 +356,15 @@
                 else:
                     near_out[i] += part
 
-            @pl.when(g == 0)
-            def _():
-                finish_stage(n)
-                start_stage(n + 1)
+            if n < 2:
+
+                @pl.when(g == 0)
+                def _():
+                    next_stage(n)
 
     @pl.when(own_limit < 2)
     def _():
-        finish_stage(1)
-        start_stage(2)
+        next_stage(1)
 
     for copy in moments:
         copy.wait_recv()

time: 35.5 us -> 37.4 us (1.054); the launches traced: 34.9 us -> 37.3 us
  Pallas kernels: 34.9 us -> 37.2 us
    pallas_call x1, Pallas kernels: 20.6 us -> 23 us  [local(): pl.pallas_call(exchange_kernel, out_shape=(pltpu.VMEM((3 * LEAVES + 1, TE...]
where the time goes in v9:
time: 37.4 us; the launch traced here: 37.3 us
  Pallas kernels  37.2 us (99%)
    pallas_call x1, Pallas kernels, local(): pl.pallas_call(exchange_kernel, out_shape=(pltpu.VMEM((3 * LEAVES + 1, TE...  23 us
    pallas_call x1, Pallas kernels, local(): pl.pallas_call(local_kernel, out_shape=(jax.ShapeDtypeStruct((LEAVES, POI...  14.3 us

profile of v9, /device:TPU:1, one launch (start us, length us, event | category | flops | bytes accessed | tf_op | source)
XLA Modules:
  0.0 37.3 jit_solution(6844441248120077078)
XLA Ops:
  0.0 23.0 %exchange.1 = (bf16[193,32,256]{2,1,0:T(8,128)(2,1)S(1)}, bf16[64,256,32]{2,1,0:T(8,128)(2,1)S(1)}, f32[200,256]{1,0:T(8,128)S(1)}, f32[128,1,128]{2,1,0:T(1,128...) custom-call(f32[64,256]{1,0:T(8,128)} %charges_hbm.1, ...), custom_call_target="tpu_custom_call" | custom-call | tf_op jit(solution)/shard_map/exchange/pallas_call | solution.py:554
  23.0 14.3 %local.1 = (f32[64,256]{1,0:T(8,128)}, f32[64,256,128]{2,1,0:T(8,128)S(1)}, f32[64,64,64]{2,1,0:T(8,128)S(1)}) custom-call(bf16[193,32,256]{2,1,0:T(8,128)(2,1)S(1)} %get-tuple-element.17.source, bf16[64,256,32]{2,1,0:T(8,128)(2,1)S(1)} %get-tuple-element.18.target, ...), custom_call_target="tpu_custom_call", output_to_operand_aliasing={{1}: (7, {}), {2}: (8, {})} | custom-call | tf_op jit(solution)/shard_map/local/pallas_call | solution.py:611

commit v10 on v8

--- a/solution.py
+++ b/solution.py
@@ -351,7 +351,7 @@
                 else:
                     near_out[i] += part
 
-            @pl.when(g == 0)
+            @pl.when(g == jnp.where(own_limit > 1, 1, 0))
             def _():
                 finish_stage(n)
                 start_stage(n + 1)

time: 35.5 us -> 34.3 us (0.966)
  Pallas kernels: 34.9 us -> 33.7 us
    pallas_call x1, Pallas kernels: 20.6 us -> 19.4 us  [local(): pl.pallas_call(exchange_kernel, out_shape=(pltpu.VMEM((3 * LEAVES + 1, TE...]
where the time goes in v10:
time: 34.3 us; the launch traced here: 33.7 us
  Pallas kernels  33.7 us (98%)
    pallas_call x1, Pallas kernels, local(): pl.pallas_call(exchange_kernel, out_shape=(pltpu.VMEM((3 * LEAVES + 1, TE...  19.4 us
    pallas_call x1, Pallas kernels, local(): pl.pallas_call(local_kernel, out_shape=(jax.ShapeDtypeStruct((LEAVES, POI...  14.3 us

profile of v10, /device:TPU:1, one launch (start us, length us, event | category | flops | bytes accessed | tf_op | source)
XLA Modules:
  0.0 33.7 jit_solution(16293365612460721984)
XLA Ops:
  0.0 19.4 %exchange.1 = (bf16[193,32,256]{2,1,0:T(8,128)(2,1)S(1)}, bf16[64,256,32]{2,1,0:T(8,128)(2,1)S(1)}, f32[200,256]{1,0:T(8,128)S(1)}, f32[128,1,128]{2,1,0:T(1,128...) custom-call(f32[64,256]{1,0:T(8,128)} %charges_hbm.1, ...), custom_call_target="tpu_custom_call" | custom-call | tf_op jit(solution)/shard_map/exchange/pallas_call | solution.py:549
  19.4 14.3 %local.1 = (f32[64,256]{1,0:T(8,128)}, f32[64,256,128]{2,1,0:T(8,128)S(1)}, f32[64,64,64]{2,1,0:T(8,128)S(1)}) custom-call(bf16[193,32,256]{2,1,0:T(8,128)(2,1)S(1)} %get-tuple-element.17.source, bf16[64,256,32]{2,1,0:T(8,128)(2,1)S(1)} %get-tuple-element.18.target, ...), custom_call_target="tpu_custom_call", output_to_operand_aliasing={{1}: (7, {}), {2}: (8, {})} | custom-call | tf_op jit(solution)/shard_map/local/pallas_call | solution.py:606

commit v11 on v10

--- a/solution.py
+++ b/solution.py
@@ -326,12 +326,12 @@
             )
         return copies
 
+    for copies in copies_of_halo[1:]:
+        for copy in copies:
+            copy.start()
     moments = moment_copies()
     for copy in moments:
         copy.start()
-    for copies in copies_of_halo[1:]:
-        for copy in copies:
-            copy.start()
 
     pl.loop(terms_before, chunks)(own_terms)
 
@@ -361,6 +361,19 @@
         finish_stage(1)
         start_stage(2)
 
+    def neighbour_terms(part):
+        for side in range(2):
+            copies_of_halo[part][side].wait_recv()
+            first = 2 * LEAVES * side
+
+            @pl.loop(part * part_leaves // CHUNK, (part + 1) * part_leaves // CHUNK)
+            def _(c):
+                span = pl.ds(pl.multiple_of(c * CHUNK, CHUNK), CHUNK)
+                parts, norm = centred([halo[side, n, span, :] for n in range(1, 4)])
+                source_out[pl.ds(first + c * CHUNK, CHUNK)] = by_leaf(source_terms(parts, norm)).astype(BF16)
+
+    neighbour_terms(0)
+
     for copy in moments:
         copy.wait_recv()
     for n in range(5):
@@ -385,17 +398,7 @@
 
     far_chunks(0, 4)
 
-    for part in range(HALO_PARTS):
-        for side in range(2):
-            copies_of_halo[part][side].wait_recv()
-            first = 2 * LEAVES * side
-
-            @pl.loop(part * part_leaves // CHUNK, (part + 1) * part_leaves // CHUNK)
-            def _(c):
-                span = pl.ds(pl.multiple_of(c * CHUNK, CHUNK), CHUNK)
-                parts, norm = centred([halo[side, n, span, :] for n in range(1, 4)])
-                source_out[pl.ds(first + c * CHUNK, CHUNK)] = by_leaf(source_terms(parts, norm)).astype(BF16)
-
+    neighbour_terms(1)
     charge_out[0:LEAVES] = halo[0, 0]
     charge_out[2 * LEAVES : 3 * LEAVES] = halo[1, 0]
 

time: 34.3 us -> 35.1 us (1.023); the launches traced: 33.7 us -> 35 us
  Pallas kernels: 33.7 us -> 35 us
    pallas_call x1, Pallas kernels: 19.4 us -> 20.2 us  [local(): pl.pallas_call(exchange_kernel, out_shape=(pltpu.VMEM((3 * LEAVES + 1, TE...]
    pallas_call x1, Pallas kernels: 14.3 us -> 14.8 us  [local(): pl.pallas_call(local_kernel, out_shape=(jax.ShapeDtypeStruct((LEAVES, POI...]
where the time goes in v11:
time: 35.1 us; the launch traced here: 35 us
  Pallas kernels  35 us (100%)
    pallas_call x1, Pallas kernels, local(): pl.pallas_call(exchange_kernel, out_shape=(pltpu.VMEM((3 * LEAVES + 1, TE...  20.2 us
    pallas_call x1, Pallas kernels, local(): pl.pallas_call(local_kernel, out_shape=(jax.ShapeDtypeStruct((LEAVES, POI...  14.8 us

profile of v11, /device:TPU:1, one launch (start us, length us, event | category | flops | bytes accessed | tf_op | source)
XLA Modules:
  0.0 35.0 jit_solution(11252627802734447711)
XLA Ops:
  0.0 20.2 %exchange.1 = (bf16[193,32,256]{2,1,0:T(8,128)(2,1)S(1)}, bf16[64,256,32]{2,1,0:T(8,128)(2,1)S(1)}, f32[200,256]{1,0:T(8,128)S(1)}, f32[128,1,128]{2,1,0:T(1,128...) custom-call(f32[64,256]{1,0:T(8,128)} %charges_hbm.1, ...), custom_call_target="tpu_custom_call" | custom-call | tf_op jit(solution)/shard_map/exchange/pallas_call | solution.py:552
  20.2 14.8 %local.1 = (f32[64,256]{1,0:T(8,128)}, f32[64,256,128]{2,1,0:T(8,128)S(1)}, f32[64,64,64]{2,1,0:T(8,128)S(1)}) custom-call(bf16[193,32,256]{2,1,0:T(8,128)(2,1)S(1)} %get-tuple-element.17.source, bf16[64,256,32]{2,1,0:T(8,128)(2,1)S(1)} %get-tuple-element.18.target, ...), custom_call_target="tpu_custom_call", output_to_operand_aliasing={{1}: (7, {}), {2}: (8, {})} | custom-call | tf_op jit(solution)/shard_map/local/pallas_call | solution.py:609
